TPU v7x, 32 devices: a whole 2x2x4 slice. The times are simulated.
32 devices in a mesh: parts: 2 (over x), tile: 16 (over z, y, core).
Axes of the slice: x: 2, y: 2, z: 4, core: 2. Of those that a mesh axis runs over, the one named last changes fastest.
Arguments:
- visibility: float32 [2048, 2, 128], P(('parts', 'tile')), parts along dimension 0, may hold values from -0.5 to 0.5
- coords: float32 [2048, 3, 128], P(('parts', 'tile')), parts along dimension 0, may hold values from -8 to 8
- block_owner: int32 [2048, 1], P(('parts', 'tile')), parts along dimension 0, may hold values from 0 to 15; in each aligned block of 64 rows (0 to 63, 64 to 127, ...) at most 8 rows name the same one
- block_row: int32 [2048], P(('parts', 'tile')), parts along dimension 0, may hold values from 0 to 96, as said below
- block_col: int32 [2048], P(('parts', 'tile')), parts along dimension 0, may hold values from 0 to 2016
- stations: int32 [2048, 2], P(('parts', 'tile')), parts along dimension 0, may hold values from 0 to 511
- block_count: int32 [32], P(('parts', 'tile')), parts along dimension 0, may hold values from 32 to 64, as said below
- beam_terms: float32 [512, 2, 1024], replicated, may hold values from -4 to 4
Outputs:
- spectrum: float32 [2, 256, 32768], P(None, ('parts', 'tile')), parts along dimension 1
There are 2 independent parts, one for each index of `parts`. A program takes and returns all parts, laid end to end along the dimension named above; an argument that names none is the same for every part. Nothing has to cross between parts.
Inputs may be any that keep to these rules, and one draw needn't show every extreme that they name: `block_owner`: among the 64 block slots of one device, at most 8 name the same owner, and every owner is named by some slot. `block_count`: some device's count is 64 in every draw. Among the 64 block slots of one device, at most 5 have the same block_row div 8.
All inputs are finite; a program needn't handle non-finite values.
Results may differ from a plain program's by a relative error of at most 0.0003.
Values sent between devices are 32-bit elements; how exact they have to be, the bound alone decides.
No kernel may reach another device: no remote copies, remote signals or barrier semaphores. Data moves between devices by JAX's collectives and lax.ppermute only.
A program may use at most 64 MiB of HBM per device.

v0:
```python
import functools
import math

import jax
import jax.numpy as jnp
import ml_dtypes
import numpy as np
from jax import lax
from jax.experimental import pallas as pl
from jax.experimental.pallas import tpu as pltpu
from jax.sharding import PartitionSpec as P

VROWS = 128
SUB = 32
NG = 32768
ROWS_DEV = 8
LEAD = 256
TAIL = 128
GROUP = 16

SIN_TERMS = (4.442879549, -7.307815317, 3.597759608, -0.791160565)
COS_TERMS = (1.414213500, -6.978850910, 5.739459580, -1.883552820, 0.310677860)


def halves(table):
    table = np.round(table, 12).astype(np.float32)
    high = table.astype(ml_dtypes.bfloat16)
    low = (table - high.astype(np.float32)).astype(ml_dtypes.bfloat16)
    return high, low


def root(numbers, length):
    angle = 2.0 * np.pi / length * (numbers % length)
    return np.cos(angle), -np.sin(angle)


def complex_left(re, im):
    return np.block([[re, -im], [im, re]])


@functools.cache
def image_tables():
    eight = np.arange(8)
    re, im = root(np.outer(eight, eight), 8)
    left = complex_left(np.kron(np.eye(GROUP), re), np.kron(np.eye(GROUP), im))
    lane = np.arange(128)
    twist = root(np.outer(eight, lane // SUB), SUB)
    four = 8 * np.outer(lane // SUB, lane // SUB) + np.outer(lane % SUB, lane % SUB)
    re, im = root(four, SUB)
    right = complex_left(re, im).T
    row_pos = ((4 * eight[:, None] + lane[None, :] // SUB) - SUB // 2) / SUB
    col_pos = np.broadcast_to((lane[None, :] % SUB - SUB // 2) / SUB, (8, 128))
    taper = (1 - 2 * row_pos**2) * (1 - 2 * col_pos**2) / SUB
    small = np.stack([taper, np.round(twist[0], 12), np.round(twist[1], 12)]).astype(np.float32)
    return (*halves(left), *halves(right), small)


@functools.cache
def row_tables():
    lead, tail = np.arange(LEAD), np.arange(TAIL)
    even = complex_left(*root(np.outer(tail, tail), TAIL))
    odd = complex_left(*root(np.outer(tail, 2 * tail + 1), LEAD))
    twist = np.stack(root(np.outer(lead, tail), NG)) / math.sqrt(NG)
    first = np.stack(halves(even) + halves(odd))
    return first, np.stack(halves(even)), np.round(twist, 12).astype(np.float32)


def split(value):
    high = value.astype(jnp.bfloat16)
    return high, (value - high.astype(jnp.float32)).astype(jnp.bfloat16)


def dot(left, right, transposed=False):
    dims = (((1,), (1 if transposed else 0,)), ((), ()))
    return lax.dot_general(left, right, dims, preferred_element_type=jnp.float32)


def table_times(table_hi, table_lo, hi, lo, transposed=False):
    rows = table_hi.shape[0]
    both = dot(jnp.concatenate([table_hi, table_lo], axis=0), hi, transposed)
    return both[:rows] + both[rows:] + dot(table_hi, lo, transposed)


def times_table(hi, lo, table_hi, table_lo):
    rows = hi.shape[0]
    both = dot(jnp.concatenate([hi, lo], axis=0), table_hi)
    return both[:rows] + both[rows:] + dot(hi, table_lo)


def polynomial(terms, z):
    value = z * terms[-1] + terms[-2]
    for term in terms[-3::-1]:
        value = value * z + term
    return value


def cos_sin(turns):
    whole = (turns + 12582912.0) - 12582912.0
    t = turns - whole
    z = t * t
    half_sin = t * polynomial(SIN_TERMS, z)
    half_cos = polynomial(COS_TERMS, z)
    return 1.0 - half_sin * half_sin, half_sin * half_cos


def send_layout(per_device, owners):
    cap = -(-per_device // (owners - SUB // ROWS_DEV + 1))
    tiles = 2 * cap + (2 * cap + 1 + 3) // 4
    return cap, tiles


def exchange_order(chips):
    quarter = chips // 4
    far = [k + part for k in range(quarter) for part in (3 * quarter, 2 * quarter)]
    near = list(range(chips // 2 - 1, 0, -1))
    return [0] + far[:3] + near[:1] + far[3:] + near[1:]


def image_kernel(
    cap,
    tile_cols,
    *refs,
):
    me = lax.axis_index("tile")
    owners = lax.axis_size("tile")
    count_s, beams, args, keep, give = refs[0], refs[1], refs[2:13], refs[13], refs[14]
    copied, (out, beam_buf, sky, ranks, sems, arg_sems) = refs[15:26], refs[26:]
    copies = [
        pltpu.make_async_copy(arg, held, arg_sems.at[k])
        for k, (arg, held) in enumerate(zip(args, copied))
    ]
    for copy in copies:
        copy.start()
    owner_s, row_s, col_s, station_s, vis, coords = copied[:6]
    left_hi, left_lo, right_hi, right_lo, small = copied[6:]
    per_device = vis.shape[0] // 2
    label_tile = 2 * cap + (2 * cap) // 4
    label_lane = SUB * ((2 * cap) % 4)
    sublane = lax.broadcasted_iota(jnp.int32, (8, 128), 0)
    lane = lax.broadcasted_iota(jnp.int32, (8, 128), 1)
    lane_group = lane // SUB
    out[...] = jnp.zeros_like(out)
    spread_columns = ((lane - label_lane) * (NG // SUB)).astype(jnp.float32)
    is_label = (sublane == 0) & (lane >= label_lane) & (lane < label_lane + SUB)
    for d in range(owners):
        out[d, label_tile] = jnp.where(is_label, spread_columns, 0.0)
    sky[...] = jnp.zeros_like(sky)
    for b in range(owners):
        ranks[b] = 0
    copies[3].wait()
    copies[1].wait()
    live = count_s[0]
    groups = (live + GROUP - 1) >> (GROUP.bit_length() - 1)

    def fetch_beams(g):
        for j in range(GROUP):
            n = jnp.minimum(g, per_device // GROUP - 1) * GROUP + j
            for side in range(2):
                pltpu.make_async_copy(
                    beams.at[station_s[side, n]],
                    beam_buf.at[2 * (g * GROUP + j) + side],
                    sems.at[g],
                ).start()

    def await_beams(g):
        waited = beam_buf.at[pl.ds(g * 2 * GROUP, 2 * GROUP)]
        pltpu.make_async_copy(beams.at[pl.ds(0, 2 * GROUP)], waited, sems.at[g]).wait()

    for g in range(2):
        fetch_beams(g)
    copies[4].wait()
    copies[5].wait()
    copies[10].wait()

    @pl.loop(0, groups * (GROUP // 8))
    def _(g):
        for j in range(8):
            n = g * 8 + j
            shift = row_s[n] & 7
            coords[0, pl.ds(n, 1), :] += shift.astype(jnp.float32)
            vis[pl.ds(2 * n, 2), :] *= (1 - 2 * (shift & 1)).astype(jnp.float32)

    taper = small[0]
    twist_re = jnp.concatenate([small[1]] * GROUP, axis=0)
    twist_im = jnp.concatenate([small[2]] * GROUP, axis=0)
    number = lax.broadcasted_iota(jnp.int32, (SUB, VROWS), 0)
    l_row = (4 * (number % 8) + number // 8 - SUB // 2).astype(jnp.float32) / SUB
    l_col = (number - SUB // 2).astype(jnp.float32) / SUB
    d_row = l_row * l_row
    d_col = l_col * l_col

    def images(g, first=False):
        for quad in range(GROUP // 4):
            x_hi, x_lo, columns = [], [], []
            for j in range(4):
                n = g * GROUP + quad * 4 + j
                u = coords[0, pl.ds(n, 1), :]
                v = coords[1, pl.ds(n, 1), :]
                w = coords[2, pl.ds(n, 1), :]
                vis_re = vis[pl.ds(2 * n, 1), :]
                vis_im = vis[pl.ds(2 * n + 1, 1), :]
                cos_row, sin_row = cos_sin(u * l_row + w * d_row)
                cos_col, sin_col = cos_sin(v * l_col + w * d_col)
                x = jnp.concatenate(
                    [
                        vis_re * cos_row - vis_im * sin_row,
                        vis_re * sin_row + vis_im * cos_row,
                    ],
                    axis=1,
                )
                hi, lo = split(x)
                x_hi.append(hi)
                x_lo.append(lo)
                columns.append(split(cos_col) + split(sin_col))
            c_hi, c_lo, s_hi, s_lo = zip(*columns)

            def matrix(c, s):
                real = [jnp.concatenate([a, -b], axis=1) for a, b in zip(c, s)]
                imag = [jnp.concatenate([b, a], axis=1) for a, b in zip(c, s)]
                return jnp.concatenate(real + imag, axis=0)

            lhs = jnp.concatenate(x_hi + x_lo, axis=0)
            both = dot(lhs, matrix(c_hi, s_hi), True)
            sums = both[:128] + both[128:] + dot(lhs[:128], matrix(c_lo, s_lo), True)
            if first and quad == 0:
                await_beams(g)
            for j in range(4):
                n = g * GROUP + quad * 4 + j
                flat = []
                for c in range(2):
                    value = None
                    for i in range(4):
                        piece = sums[32 * j + 8 * i : 32 * j + 8 * i + 8, 128 * c : 128 * c + 128]
                        if i != j:
                            piece = pltpu.roll(piece, (SUB * (i - j)) % 128, 1)
                        value = piece if value is None else jnp.where(lane_group == i, piece, value)
                    flat.append(value)
                one_re = beam_buf[2 * n, pl.ds(0, 8, stride=2), :]
                one_im = beam_buf[2 * n, pl.ds(1, 8, stride=2), :]
                two_re = beam_buf[2 * n + 1, pl.ds(0, 8, stride=2), :]
                two_im = beam_buf[2 * n + 1, pl.ds(1, 8, stride=2), :]
                beam_re = taper * (one_re * two_re + one_im * two_im)
                beam_im = taper * (one_im * two_re - one_re * two_im)
                sky_re = beam_re * flat[0] - beam_im * flat[1]
                sky_im = beam_re * flat[1] + beam_im * flat[0]
                in_use = n < live
                place = (quad * 4 + j) * 8
                sky[g & 1, place : place + 8, :] = jnp.where(in_use, sky_re, 0.0)
                sky[g & 1, place + 8 * GROUP : place + 8 * GROUP + 8, :] = jnp.where(in_use, sky_im, 0.0)

    def cells(g):
        hi, lo = split(sky[g & 1])
        z = table_times(left_hi[...], left_lo[...], hi, lo)
        z_re, z_im = z[: 8 * GROUP], z[8 * GROUP :]
        y_re = z_re * twist_re - z_im * twist_im
        y_im = z_re * twist_im + z_im * twist_re
        hi, lo = split(jnp.concatenate([y_re, y_im], axis=1))
        result = times_table(hi, lo, right_hi[...], right_lo[...])
        for j in range(GROUP):
            n = g * GROUP + j
            band = row_s[n] >> 3
            shift = row_s[n] & 7
            rank = ranks[band]
            ranks[band] = rank + 1
            late = sublane < shift
            last = jnp.minimum(band + 4, owners - 1)
            for c in range(2):
                value = result[8 * j : 8 * j + 8, 128 * c : 128 * c + 128]
                spread = jnp.where(late & (lane_group == 0), 0.0, value)
                tile = 2 * rank + c
                for o in range(4):
                    pltpu.store(out.at[(band + o) ^ me, tile], spread, mask=lane_group == o)
                part = tile & 3
                tail = pltpu.roll(value, SUB * part, 1)
                pltpu.store(
                    out.at[last ^ me, 2 * cap + (tile >> 2)], tail, mask=late & (lane_group == part)
                )
            column = jnp.full((8, 128), owner_s[n] * tile_cols + col_s[n], jnp.float32)
            for o in range(5):
                here = (sublane == 0) & (lane == label_lane + o * cap + rank)
                if o == 4:
                    here = here & (sublane < shift)
                target = last if o == 4 else band + o
                pltpu.store(out.at[target ^ me, label_tile], column, mask=here)

    images(0, True)
    for copy in copies[6:10] + [copies[0], copies[2]]:
        copy.wait()

    @pl.loop(1, groups)
    def _(g):
        await_beams(g)
        fetch_beams(g + 1)
        cells(g - 1)
        images(g)

    cells(groups - 1)
    await_beams(groups)
    for k in range(owners // 2):
        keep[k] = out[2 * k]
        give[k] = out[2 * k + 1]


def merge_kernel(keep, got, *messages):
    for k, message in zip(exchange_order(keep.shape[0]), messages):
        message[0] = keep[k]
        message[1] = got[k]


def row_kernel(
    cap,
    first,
    second,
    twist,
    *refs,
):
    sources = lax.axis_size("tile")
    messages, out, received = refs[: sources // 2], refs[sources // 2], refs[sources // 2 + 1]
    scratch = refs[sources // 2 + 2 :]
    grids, (label_v, label_s, sem, middle, held, out_sems) = scratch[:2], scratch[2:]
    for k, message in enumerate(messages):
        received[2 * k] = message[0]
        received[2 * k + 1] = message[1]
    label_tile = 2 * cap + (2 * cap) // 4
    label_lane = SUB * ((2 * cap) % 4)
    label_v[...] = received[:, label_tile, 0, :].astype(jnp.int32)
    copy = pltpu.make_async_copy(label_v, label_s, sem)
    copy.start()
    for grid in grids:
        grid[...] = jnp.zeros_like(grid)
    lane = lax.broadcasted_iota(jnp.int32, (8, 128), 1)
    copy.wait()

    @pl.loop(0, sources)
    def _(source):
        for i in range(cap):
            for o in range(5):
                column = label_s[source, label_lane + o * cap + i]
                offset = column & 127
                here = pl.multiple_of((column >> 7) * 8, 8)
                place = lane - offset
                inside = (place >= 0) & (place < SUB)
                beyond = place < SUB - 128
                added = []
                for c in range(2):
                    if o < 4:
                        value, part = received[source, 2 * i + c], o
                    else:
                        value = received[source, 2 * cap + (2 * i + c) // 4]
                        part = (2 * i + c) % 4
                    value = pltpu.roll(value, (offset - SUB * part) & 127, 1)
                    added.append(jnp.where(inside, value, 0.0))
                    added.append(jnp.where(beyond, value, 0.0))
                before = [
                    grids[c][pl.ds(here + 8 * k, 8), :] for c in range(2) for k in range(2)
                ]
                for c in range(2):
                    for k in range(2):
                        grids[c][pl.ds(here + 8 * k, 8), :] = before[2 * c + k] + added[2 * c + k]

    for pair in range(ROWS_DEV // 2):
        halves_of = []
        for e in range(2):
            rows = [
                pl.ds(ROWS_DEV * e + 2 * pair + k, TAIL, stride=2 * ROWS_DEV) for k in range(2)
            ]
            value = jnp.concatenate(
                [jnp.concatenate([grids[c][at, :] for at in rows], axis=1) for c in range(2)], 0
            )
            hi, lo = split(value)
            halves_of.append(table_times(first[2 * e], first[2 * e + 1], hi, lo))
        for h, a in enumerate((halves_of[0] + halves_of[1], halves_of[0] - halves_of[1])):
            turn_re = twist[0, TAIL * h : TAIL * h + TAIL]
            turn_im = twist[1, TAIL * h : TAIL * h + TAIL]
            for k in range(2):
                a_re = a[:TAIL, 128 * k : 128 * k + 128]
                a_im = a[TAIL:, 128 * k : 128 * k + 128]
                b = jnp.concatenate(
                    [a_re * turn_re - a_im * turn_im, a_re * turn_im + a_im * turn_re], axis=1
                )
                for part, value in enumerate(split(b)):
                    middle[h, pair, part, TAIL * k : TAIL * k + TAIL, :] = value

    copies = []
    for h in range(2):
        for pair in range(ROWS_DEV // 2):
            result = table_times(
                second[0], second[1], middle[h, pair, 0], middle[h, pair, 1], True
            )
            for c in range(2):
                for k in range(2):
                    held[h, c, pl.ds(2 * pair + k, TAIL, stride=ROWS_DEV), :] = result[
                        128 * c : 128 * c + 128, 128 * k : 128 * k + 128
                    ]
        for c in range(2):
            copies.append(
                pltpu.make_async_copy(
                    held.at[h, c].reshape(TAIL, ROWS_DEV, TAIL),
                    out.at[c, :, h],
                    out_sems.at[h, c],
                )
            )
            copies[-1].start()
    for copy in copies:
        copy.wait()


def shards(
    visibility, coords, block_owner, block_row, block_col, stations, block_count, beam_terms
):
    owners = lax.axis_size("tile")
    per_device = visibility.shape[0]
    tile_cols = NG // owners
    cap, tiles = send_layout(per_device, owners)
    stations_all = beam_terms.shape[0]
    vmem = pl.BlockSpec(memory_space=pltpu.VMEM)
    beams = (
        beam_terms.reshape(stations_all, 2, 8, 128)
        .transpose(0, 2, 1, 3)
        .reshape(stations_all, 16, 128)
    )
    labels = (
        block_owner.reshape(per_device),
        block_row,
        block_col,
        stations.T,
    )
    values = (
        visibility.reshape(per_device * 2, VROWS),
        coords.transpose(1, 0, 2),
        *image_tables(),
    )
    hbm = pl.BlockSpec(memory_space=pltpu.HBM)
    half = jax.ShapeDtypeStruct((owners // 2, tiles, 8, 128), jnp.float32)
    keep, give = pl.pallas_call(
        functools.partial(image_kernel, cap, tile_cols),
        out_shape=[half] * 2,
        in_specs=[pl.BlockSpec(memory_space=pltpu.SMEM)] + [hbm] * (1 + len(labels) + len(values)),
        out_specs=[vmem] * 2,
        scratch_shapes=[
            *(pltpu.SMEM(label.shape, label.dtype) for label in labels),
            *(pltpu.VMEM(value.shape, value.dtype) for value in values),
            pltpu.VMEM((owners, tiles, 8, 128), jnp.float32),
            pltpu.VMEM((2 * (per_device + GROUP), 16, 128), jnp.float32),
            pltpu.VMEM((2, 16 * GROUP, 128), jnp.float32),
            pltpu.SMEM((owners,), jnp.int32),
            pltpu.SemaphoreType.DMA((per_device // GROUP + 1,)),
            pltpu.SemaphoreType.DMA((len(labels) + len(values),)),
        ],
        compiler_params=pltpu.CompilerParams(vmem_limit_bytes=24 * 1024 * 1024),
        name="image",
    )(
        block_count,
        *(pltpu.with_memory_space_constraint(x, pltpu.HBM) for x in (beams, *labels, *values)),
    )
    got = lax.ppermute(give, "tile", [(source, source ^ 1) for source in range(owners)])
    messages = pl.pallas_call(
        merge_kernel,
        out_shape=[jax.ShapeDtypeStruct((2, tiles, 8, 128), jnp.float32)] * (owners // 2),
        in_specs=[vmem] * 2,
        out_specs=[vmem] * (owners // 2),
        compiler_params=pltpu.CompilerParams(vmem_limit_bytes=24 * 1024 * 1024),
        name="merge",
    )(keep, got)
    received = [messages[0]] + [
        lax.ppermute(message, "tile", [(source, source ^ (2 * k)) for source in range(owners)])
        for message, k in zip(messages[1:], exchange_order(owners // 2)[1:])
    ]
    result = pl.pallas_call(
        functools.partial(row_kernel, cap),
        out_shape=jax.ShapeDtypeStruct((2, TAIL, 2, ROWS_DEV, TAIL), jnp.float32),
        in_specs=[vmem] * (3 + owners // 2),
        out_specs=pl.BlockSpec(memory_space=pl.ANY),
        scratch_shapes=[
            pltpu.VMEM((owners, tiles, 8, 128), jnp.float32),
            *(pltpu.VMEM(((LEAD + 1) * ROWS_DEV, TAIL), jnp.float32) for _ in range(2)),
            pltpu.VMEM((owners, 128), jnp.int32),
            pltpu.SMEM((owners, 128), jnp.int32),
            pltpu.SemaphoreType.DMA,
            pltpu.VMEM((2, ROWS_DEV // 2, 2, 2 * TAIL, 2 * TAIL), jnp.bfloat16),
            pltpu.VMEM((2, 2, TAIL * ROWS_DEV, TAIL), jnp.float32),
            pltpu.SemaphoreType.DMA((2, 2)),
        ],
        compiler_params=pltpu.CompilerParams(vmem_limit_bytes=24 * 1024 * 1024),
        name="rows",
    )(*row_tables(), *received)
    return (
        result.reshape(2, LEAD, ROWS_DEV, TAIL).transpose(0, 2, 1, 3).reshape(2, ROWS_DEV, NG)
    )


def solution(mesh):
    placed = (
        P(("parts", "tile"), None, None),
        P(("parts", "tile"), None, None),
        P(("parts", "tile"), None),
        P(("parts", "tile")),
        P(("parts", "tile")),
        P(("parts", "tile"), None),
        P(("parts", "tile")),
        P(),
    )
    return jax.shard_map(
        shards,
        mesh=mesh,
        in_specs=placed,
        out_specs=P(None, ("parts", "tile"), None),
        check_vma=False,
    )
```

profile of v0, /device:TPU:0, one launch (start us, length us, event | category | flops | bytes accessed | tf_op | source)
XLA Modules:
  0.0 42.5 jit_solution(15709440756781496726)
XLA Ops:
  0.0 0.0 copy-start.1
  0.0 0.0 copy-start.2
  0.0 0.0 copy-start
  0.7 7.1 %image.1 = (f32[8,13,8,128]{3,2,1,0:T(8,128)S(1)}, f32[8,13,8,128]{3,2,1,0:T(8,128)S(1)}) custom-call(s32[1]{0:T(128)S(6)} %copy.18.refs_0_, f32[512,16,128]{2,1,0:T(8,128)} %bitcast.14, s32[64]{0:T(128)} %bitcast.18, s32[64]{0:T(128)} %refs_3_.1, s32[64]{0:T(128)} %refs_4_.1, s32[2,64]{1,0:T(2,128)} %bitcast.17, f32[128,128]{1,0:T(8,128)} %bitcast.16, ...), custom_call_target="tpu_custom_call" | custom-call | tf_op jit(solution)/shard_map/image/pallas_call | solution.py:435
  7.9 0.5 %collective-permute-start = (f32[8,13,8,128]{3,2,1,0:T(8,128)S(1)}, f32[8,13,8,128]{3,2,1,0:T(8,128)S(1)}, u32[]{:S(2)}, u32[]{:S(2)}) collective-permute-start(f32[8,13,8,128]{3,2,1,0:T(8,128)S(1)} %get-tuple-element.16), channel_id=1, source_target_pairs={{0,1},{1,0},{2,3},{3,2},{4,5},{5,4},{6,7},{7,6},{8,9},{9,8},{10,11... | collective-permute-start | bytes 1277960 | tf_op jit(solution)/shard_map/ppermute | solution.py:456
  8.4 1.4 %collective-permute-done.got = f32[8,13,8,128]{3,2,1,0:T(8,128)S(1)} collective-permute-done((f32[8,13,8,128]{3,2,1,0:T(8,128)S(1)}, f32[8,13,8,128]{3,2,1,0:T(8,128)S(1)}, u32[]{:S(2)}, u32[]{:S(2)}) %collective-permute-start) | collective-permute-done | bytes 426016 | tf_op jit(solution)/shard_map/ppermute | solution.py:456
  9.8 0.1 merge.1
  9.9 4.5 %collective-permute-start.1 = (f32[2,13,8,128]{3,2,1,0:T(8,128)S(1)}, f32[2,13,8,128]{3,2,1,0:T(8,128)S(1)}, u32[]{:S(2)}, u32[]{:S(2)}) collective-permute-start(f32[2,13,8,128]{3,2,1,0:T(8,128)S(1)} %get-tuple-element.18), channel_id=1, source_target_pairs={{0,12},{1,13},{2,14},{3,15},{4,8},{5,9},{6,10},{7,11},{8,4},{9,5},... | collective-permute-start | bytes 319496 | tf_op jit(solution)/shard_map/ppermute | solution.py:466
  14.4 0.0 collective-permute-start.2
  14.4 3.4 %collective-permute-start.3 = (f32[2,13,8,128]{3,2,1,0:T(8,128)S(1)}, f32[2,13,8,128]{3,2,1,0:T(8,128)S(1)}, u32[]{:S(2)}, u32[]{:S(2)}) collective-permute-start(f32[2,13,8,128]{3,2,1,0:T(8,128)S(1)} %get-tuple-element.20), channel_id=1, source_target_pairs={{0,14},{1,15},{2,12},{3,13},{4,10},{5,11},{6,8},{7,9},{8,6},{9,7},... | collective-permute-start | bytes 319496 | tf_op jit(solution)/shard_map/ppermute | solution.py:466
  17.8 1.0 %collective-permute-start.4 = (f32[2,13,8,128]{3,2,1,0:T(8,128)S(1)}, f32[2,13,8,128]{3,2,1,0:T(8,128)S(1)}, u32[]{:S(2)}, u32[]{:S(2)}) collective-permute-start(f32[2,13,8,128]{3,2,1,0:T(8,128)S(1)} %get-tuple-element.21), channel_id=1, source_target_pairs={{0,6},{1,7},{2,4},{3,5},{4,2},{5,3},{6,0},{7,1},{8,14},{9,15},{10,... | collective-permute-start | bytes 319496 | tf_op jit(solution)/shard_map/ppermute | solution.py:466
  18.8 2.4 %collective-permute-start.5 = (f32[2,13,8,128]{3,2,1,0:T(8,128)S(1)}, f32[2,13,8,128]{3,2,1,0:T(8,128)S(1)}, u32[]{:S(2)}, u32[]{:S(2)}) collective-permute-start(f32[2,13,8,128]{3,2,1,0:T(8,128)S(1)} %get-tuple-element.22), channel_id=1, source_target_pairs={{0,10},{1,11},{2,8},{3,9},{4,14},{5,15},{6,12},{7,13},{8,2},{9,3},... | collective-permute-start | bytes 319496 | tf_op jit(solution)/shard_map/ppermute | solution.py:466
  21.2 0.0 collective-permute-done.1.refs_1_
  21.2 4.5 %collective-permute-start.6 = (f32[2,13,8,128]{3,2,1,0:T(8,128)S(1)}, f32[2,13,8,128]{3,2,1,0:T(8,128)S(1)}, u32[]{:S(2)}, u32[]{:S(2)}) collective-permute-start(f32[2,13,8,128]{3,2,1,0:T(8,128)S(1)} %get-tuple-element.23), channel_id=1, source_target_pairs={{0,4},{1,5},{2,6},{3,7},{4,0},{5,1},{6,2},{7,3},{8,12},{9,13},{10,... | collective-permute-start | bytes 319496 | tf_op jit(solution)/shard_map/ppermute | solution.py:466
  25.7 3.3 %collective-permute-done.2.refs_2_ = f32[2,13,8,128]{3,2,1,0:T(8,128)S(1)} collective-permute-done((f32[2,13,8,128]{3,2,1,0:T(8,128)S(1)}, f32[2,13,8,128]{3,2,1,0:T(8,128)S(1)}, u32[]{:S(2)}, u32[]{:S(2)}) %collective-permute-start.2) | collective-permute-done | bytes 106528 | tf_op jit(solution)/shard_map/ppermute | solution.py:466
  29.0 2.2 %collective-permute-start.7 = (f32[2,13,8,128]{3,2,1,0:T(8,128)S(1)}, f32[2,13,8,128]{3,2,1,0:T(8,128)S(1)}, u32[]{:S(2)}, u32[]{:S(2)}) collective-permute-start(f32[2,13,8,128]{3,2,1,0:T(8,128)S(1)} %get-tuple-element.24), channel_id=1, source_target_pairs={{0,2},{1,3},{2,0},{3,1},{4,6},{5,7},{6,4},{7,5},{8,10},{9,11},{10,... | collective-permute-start | bytes 319496 | tf_op jit(solution)/shard_map/ppermute | solution.py:466
  31.2 0.0 collective-permute-done.3.refs_3_
  31.2 0.0 collective-permute-done.4.refs_4_
  31.2 3.3 %collective-permute-done.5.refs_5_ = f32[2,13,8,128]{3,2,1,0:T(8,128)S(1)} collective-permute-done((f32[2,13,8,128]{3,2,1,0:T(8,128)S(1)}, f32[2,13,8,128]{3,2,1,0:T(8,128)S(1)}, u32[]{:S(2)}, u32[]{:S(2)}) %collective-permute-start.5) | collective-permute-done | bytes 106528 | tf_op jit(solution)/shard_map/ppermute | solution.py:466
  34.5 0.0 collective-permute-done.6.refs_6_
  34.5 0.9 %collective-permute-done.7.refs_7_ = f32[2,13,8,128]{3,2,1,0:T(8,128)S(1)} collective-permute-done((f32[2,13,8,128]{3,2,1,0:T(8,128)S(1)}, f32[2,13,8,128]{3,2,1,0:T(8,128)S(1)}, u32[]{:S(2)}, u32[]{:S(2)}) %collective-permute-start.7) | collective-permute-done | bytes 106528 | tf_op jit(solution)/shard_map/ppermute | solution.py:466
  35.4 0.0 copy-done.1
  35.4 0.0 copy-done.2
  35.4 0.0 copy-done
  35.4 7.1 %rows.1 = f32[2,128,2,8,128]{4,3,2,1,0:T(8,128)} custom-call(bf16[4,256,256]{2,1,0:T(8,128)(2,1)S(1)} %copy-done, bf16[2,256,256]{2,1,0:T(8,128)(2,1)S(1)} %copy-done.2, f32[2,256,128]{2,1,0:T(8,128)S(1)} %copy-done.1, f32[2,13,8,128]{3,2,1,0:T(8,128)S(1)} %get-tuple-element.17.refs_0_, f32[2,13,8,128]{3,2,1,0:T(8,128)S(1)} %collective-permute-done.1.refs_1_, ...), custom_call_target="tpu_custom_call" | custom-call | tf_op jit(solution)/shard_map/rows/pallas_call | solution.py:469
Async XLA Ops:
  0.0 35.4 %copy-start.1 = (f32[2,256,128]{2,1,0:T(8,128)S(1)}, f32[2,256,128]{2,1,0:T(8,128)}, u32[]{:S(2)}) copy-start(f32[2,256,128]{2,1,0:T(8,128)} %constant.23.clone.twist) | copy-start | bytes 786436
  0.0 35.4 %copy-start.2 = (bf16[2,256,256]{2,1,0:T(8,128)(2,1)S(1)}, bf16[2,256,256]{2,1,0:T(8,128)(2,1)}, u32[]{:S(2)}) copy-start(bf16[2,256,256]{2,1,0:T(8,128)(2,1)} %constant.22.clone.second) | copy-start | bytes 786436
  0.0 35.4 %copy-start = (bf16[4,256,256]{2,1,0:T(8,128)(2,1)S(1)}, bf16[4,256,256]{2,1,0:T(8,128)(2,1)}, u32[]{:S(2)}) copy-start(bf16[4,256,256]{2,1,0:T(8,128)(2,1)} %constant.21.clone.first) | copy-start | bytes 1572868
  7.9 1.9 %collective-permute-start = (f32[8,13,8,128]{3,2,1,0:T(8,128)S(1)}, f32[8,13,8,128]{3,2,1,0:T(8,128)S(1)}, u32[]{:S(2)}, u32[]{:S(2)}) collective-permute-start(f32[8,13,8,128]{3,2,1,0:T(8,128)S(1)} %get-tuple-element.16), channel_id=1, source_target_pairs={{0,1},{1,0},{2,3},{3,2},{4,5},{5,4},{6,7},{7,6},{8,9},{9,8},{10,11... | collective-permute-start | bytes 1277960 | tf_op jit(solution)/shard_map/ppermute | solution.py:456
  9.9 11.3 %collective-permute-start.1 = (f32[2,13,8,128]{3,2,1,0:T(8,128)S(1)}, f32[2,13,8,128]{3,2,1,0:T(8,128)S(1)}, u32[]{:S(2)}, u32[]{:S(2)}) collective-permute-start(f32[2,13,8,128]{3,2,1,0:T(8,128)S(1)} %get-tuple-element.18), channel_id=1, source_target_pairs={{0,12},{1,13},{2,14},{3,15},{4,8},{5,9},{6,10},{7,11},{8,4},{9,5},... | collective-permute-start | bytes 319496 | tf_op jit(solution)/shard_map/ppermute | solution.py:466
  14.4 14.6 %collective-permute-start.2 = (f32[2,13,8,128]{3,2,1,0:T(8,128)S(1)}, f32[2,13,8,128]{3,2,1,0:T(8,128)S(1)}, u32[]{:S(2)}, u32[]{:S(2)}) collective-permute-start(f32[2,13,8,128]{3,2,1,0:T(8,128)S(1)} %get-tuple-element.19), channel_id=1, source_target_pairs={{0,8},{1,9},{2,10},{3,11},{4,12},{5,13},{6,14},{7,15},{8,0},{9,1},... | collective-permute-start | bytes 319496 | tf_op jit(solution)/shard_map/ppermute | solution.py:466
  14.4 16.8 %collective-permute-start.3 = (f32[2,13,8,128]{3,2,1,0:T(8,128)S(1)}, f32[2,13,8,128]{3,2,1,0:T(8,128)S(1)}, u32[]{:S(2)}, u32[]{:S(2)}) collective-permute-start(f32[2,13,8,128]{3,2,1,0:T(8,128)S(1)} %get-tuple-element.20), channel_id=1, source_target_pairs={{0,14},{1,15},{2,12},{3,13},{4,10},{5,11},{6,8},{7,9},{8,6},{9,7},... | collective-permute-start | bytes 319496 | tf_op jit(solution)/shard_map/ppermute | solution.py:466
  17.8 13.4 %collective-permute-start.4 = (f32[2,13,8,128]{3,2,1,0:T(8,128)S(1)}, f32[2,13,8,128]{3,2,1,0:T(8,128)S(1)}, u32[]{:S(2)}, u32[]{:S(2)}) collective-permute-start(f32[2,13,8,128]{3,2,1,0:T(8,128)S(1)} %get-tuple-element.21), channel_id=1, source_target_pairs={{0,6},{1,7},{2,4},{3,5},{4,2},{5,3},{6,0},{7,1},{8,14},{9,15},{10,... | collective-permute-start | bytes 319496 | tf_op jit(solution)/shard_map/ppermute | solution.py:466
  18.8 15.7 %collective-permute-start.5 = (f32[2,13,8,128]{3,2,1,0:T(8,128)S(1)}, f32[2,13,8,128]{3,2,1,0:T(8,128)S(1)}, u32[]{:S(2)}, u32[]{:S(2)}) collective-permute-start(f32[2,13,8,128]{3,2,1,0:T(8,128)S(1)} %get-tuple-element.22), channel_id=1, source_target_pairs={{0,10},{1,11},{2,8},{3,9},{4,14},{5,15},{6,12},{7,13},{8,2},{9,3},... | collective-permute-start | bytes 319496 | tf_op jit(solution)/shard_map/ppermute | solution.py:466
  21.2 13.3 %collective-permute-start.6 = (f32[2,13,8,128]{3,2,1,0:T(8,128)S(1)}, f32[2,13,8,128]{3,2,1,0:T(8,128)S(1)}, u32[]{:S(2)}, u32[]{:S(2)}) collective-permute-start(f32[2,13,8,128]{3,2,1,0:T(8,128)S(1)} %get-tuple-element.23), channel_id=1, source_target_pairs={{0,4},{1,5},{2,6},{3,7},{4,0},{5,1},{6,2},{7,3},{8,12},{9,13},{10,... | collective-permute-start | bytes 319496 | tf_op jit(solution)/shard_map/ppermute | solution.py:466
  29.0 6.4 %collective-permute-start.7 = (f32[2,13,8,128]{3,2,1,0:T(8,128)S(1)}, f32[2,13,8,128]{3,2,1,0:T(8,128)S(1)}, u32[]{:S(2)}, u32[]{:S(2)}) collective-permute-start(f32[2,13,8,128]{3,2,1,0:T(8,128)S(1)} %get-tuple-element.24), channel_id=1, source_target_pairs={{0,2},{1,3},{2,0},{3,1},{4,6},{5,7},{6,4},{7,5},{8,10},{9,11},{10,... | collective-permute-start | bytes 319496 | tf_op jit(solution)/shard_map/ppermute | solution.py:466
where the time goes:
time: 42.7 us; the launch traced here: 42.5 us
  starting transfers between devices  18.5 us (43%)
  Pallas kernels  14.3 us (33%)
  waiting for transfers between devices  8.97 us (21%)
  between operations  0.77 us (2%)
    ppermute x7, starting transfers between devices, shards(): lax.ppermute(message, 'tile', [(source, source ^ 2 * k) for source in ran...  18 us
    ppermute x7, waiting for transfers between devices, shards(): lax.ppermute(message, 'tile', [(source, source ^ 2 * k) for source in ran...  7.57 us
    pallas_call x1, Pallas kernels, shards(): pl.pallas_call(functools.partial(image_kernel, cap, tile_cols), out_shape...  7.15 us
    pallas_call x1, Pallas kernels, shards(): pl.pallas_call(functools.partial(row_kernel, cap), out_shape=jax.ShapeDty...  7.08 us
    ppermute x1, waiting for transfers between devices, shards(): lax.ppermute(give, 'tile', [(source, source ^ 1) for source in range(owne...  1.4 us
  transfers between devices with their start and end apart: 8, of which 4 were waited for; matrix products, arithmetic and copies ran while one was open for 0% of the time, Pallas kernels for 0%

commit v1 on v0

--- a/solution.py
+++ b/solution.py
@@ -307,27 +307,19 @@
         message[1] = got[k]
 
 
-def row_kernel(
-    cap,
-    first,
-    second,
-    twist,
-    *refs,
-):
-    sources = lax.axis_size("tile")
-    messages, out, received = refs[: sources // 2], refs[sources // 2], refs[sources // 2 + 1]
-    scratch = refs[sources // 2 + 2 :]
-    grids, (label_v, label_s, sem, middle, held, out_sems) = scratch[:2], scratch[2:]
+def place_slabs(cap, messages, grids, scratch, earlier=None):
+    received, label_v, label_s, sem = scratch
+    sources = 2 * len(messages)
     for k, message in enumerate(messages):
         received[2 * k] = message[0]
         received[2 * k + 1] = message[1]
     label_tile = 2 * cap + (2 * cap) // 4
     label_lane = SUB * ((2 * cap) % 4)
-    label_v[...] = received[:, label_tile, 0, :].astype(jnp.int32)
+    label_v[:sources] = received[:sources, label_tile, 0, :].astype(jnp.int32)
     copy = pltpu.make_async_copy(label_v, label_s, sem)
     copy.start()
-    for grid in grids:
-        grid[...] = jnp.zeros_like(grid)
+    for c, grid in enumerate(grids):
+        grid[...] = earlier[c][...] if earlier else jnp.zeros_like(grid)
     lane = lax.broadcasted_iota(jnp.int32, (8, 128), 1)
     copy.wait()
 
@@ -358,6 +350,24 @@
                     for k in range(2):
                         grids[c][pl.ds(here + 8 * k, 8), :] = before[2 * c + k] + added[2 * c + k]
 
+
+def early_kernel(cap, count, *refs):
+    place_slabs(cap, refs[:count], refs[count : count + 2], refs[count + 2 :])
+
+
+def row_kernel(
+    cap,
+    count,
+    first,
+    second,
+    twist,
+    *refs,
+):
+    earlier, messages, out = refs[:2], refs[2 : 2 + count], refs[2 + count]
+    grids, scratch = refs[3 + count : 5 + count], refs[5 + count :]
+    middle, held, out_sems = scratch[4:]
+    place_slabs(cap, messages, grids, scratch[:4], earlier)
+
     for pair in range(ROWS_DEV // 2):
         halves_of = []
         for e in range(2):
@@ -466,24 +476,40 @@
         lax.ppermute(message, "tile", [(source, source ^ (2 * k)) for source in range(owners)])
         for message, k in zip(messages[1:], exchange_order(owners // 2)[1:])
     ]
+    early = min(5, owners // 2)
+    late = owners // 2 - early
+    grid = jax.ShapeDtypeStruct(((LEAD + 1) * ROWS_DEV, TAIL), jnp.float32)
+    placing = [
+        pltpu.VMEM((owners, tiles, 8, 128), jnp.float32),
+        pltpu.VMEM((owners, 128), jnp.int32),
+        pltpu.SMEM((owners, 128), jnp.int32),
+        pltpu.SemaphoreType.DMA,
+    ]
+    grids = pl.pallas_call(
+        functools.partial(early_kernel, cap, early),
+        out_shape=[grid] * 2,
+        in_specs=[vmem] * early,
+        out_specs=[vmem] * 2,
+        scratch_shapes=placing,
+        cost_estimate=pl.CostEstimate(flops=3 * 10**9, bytes_accessed=10**7, transcendentals=0),
+        compiler_params=pltpu.CompilerParams(vmem_limit_bytes=24 * 1024 * 1024),
+        name="early",
+    )(*received[:early])
     result = pl.pallas_call(
-        functools.partial(row_kernel, cap),
+        functools.partial(row_kernel, cap, late),
         out_shape=jax.ShapeDtypeStruct((2, TAIL, 2, ROWS_DEV, TAIL), jnp.float32),
-        in_specs=[vmem] * (3 + owners // 2),
+        in_specs=[vmem] * (5 + late),
         out_specs=pl.BlockSpec(memory_space=pl.ANY),
         scratch_shapes=[
-            pltpu.VMEM((owners, tiles, 8, 128), jnp.float32),
-            *(pltpu.VMEM(((LEAD + 1) * ROWS_DEV, TAIL), jnp.float32) for _ in range(2)),
-            pltpu.VMEM((owners, 128), jnp.int32),
-            pltpu.SMEM((owners, 128), jnp.int32),
-            pltpu.SemaphoreType.DMA,
+            *(pltpu.VMEM(grid.shape, grid.dtype) for _ in range(2)),
+            *placing,
             pltpu.VMEM((2, ROWS_DEV // 2, 2, 2 * TAIL, 2 * TAIL), jnp.bfloat16),
             pltpu.VMEM((2, 2, TAIL * ROWS_DEV, TAIL), jnp.float32),
             pltpu.SemaphoreType.DMA((2, 2)),
         ],
         compiler_params=pltpu.CompilerParams(vmem_limit_bytes=24 * 1024 * 1024),
         name="rows",
-    )(*row_tables(), *received)
+    )(*row_tables(), *grids, *received[early:])
     return (
         result.reshape(2, LEAD, ROWS_DEV, TAIL).transpose(0, 2, 1, 3).reshape(2, ROWS_DEV, NG)
     )

time: 42.7 us -> 40.8 us (0.956)
  waiting for transfers between devices: 8.97 us -> 6.52 us
  Pallas kernels: 14.3 us -> 15.1 us
    ppermute x7, waiting for transfers between devices: 7.57 us -> 4.76 us  [shards(): lax.ppermute(message, 'tile', [(source, source ^ 2 * k) for source in ran...]
    pallas_call x1 -> x2, Pallas kernels: 7.08 us -> 7.94 us  [the longest x1 5.25 us: shards(): pl.pallas_call(functools.partial(row_kernel, cap, late), out_shape=jax.Sh...]
    ppermute x1, starting transfers between devices: 0.52 us -> 0.07 us  [shards(): lax.ppermute(give, 'tile', [(source, source ^ 1) for source in range(owne...]
  transfers between devices with their start and end apart: 8 -> 8, of which waited for: 4 -> 4; matrix products, arithmetic and copies ran while one was open for 0% -> 0% of each run, Pallas kernels for 0% -> 7%
where the time goes in v1:
time: 40.8 us; the launch traced here: 40.6 us
  starting transfers between devices  18.2 us (45%)
  Pallas kernels  15.1 us (37%)
  waiting for transfers between devices  6.52 us (16%)
  between operations  0.71 us (2%)
    ppermute x7, starting transfers between devices, shards(): lax.ppermute(message, 'tile', [(source, source ^ 2 * k) for source in ran...  18.1 us
    pallas_call x1, Pallas kernels, shards(): pl.pallas_call(functools.partial(image_kernel, cap, tile_cols), out_shape...  7.15 us
    pallas_call x1, Pallas kernels, shards(): pl.pallas_call(functools.partial(row_kernel, cap, late), out_shape=jax.Sh...  5.25 us
    ppermute x7, waiting for transfers between devices, shards(): lax.ppermute(message, 'tile', [(source, source ^ 2 * k) for source in ran...  4.76 us
    pallas_call x1, Pallas kernels, shards(): pl.pallas_call(functools.partial(early_kernel, cap, early), out_shape=[gr...  2.69 us
    ppermute x1, waiting for transfers between devices, shards(): lax.ppermute(give, 'tile', [(source, source ^ 1) for source in range(owne...  1.76 us
  transfers between devices with their start and end apart: 8, of which 4 were waited for; matrix products, arithmetic and copies ran while one was open for 0% of the time, Pallas kernels for 7%

profile of v1, /device:TPU:0, one launch (start us, length us, event | category | flops | bytes accessed | tf_op | source)
XLA Modules:
  0.0 40.6 jit_solution(11789869200253486168)
XLA Ops:
  0.7 7.1 %image.1 = (f32[8,13,8,128]{3,2,1,0:T(8,128)S(1)}, f32[8,13,8,128]{3,2,1,0:T(8,128)S(1)}) custom-call(s32[1]{0:T(128)S(6)} %copy.18.refs_0_, f32[512,16,128]{2,1,0:T(8,128)} %bitcast.14, s32[64]{0:T(128)} %bitcast.18, s32[64]{0:T(128)} %refs_3_.1, s32[64]{0:T(128)} %refs_4_.1, s32[2,64]{1,0:T(2,128)} %bitcast.17, f32[128,128]{1,0:T(8,128)} %bitcast.16, ...), custom_call_target="tpu_custom_call" | custom-call | tf_op jit(solution)/shard_map/image/pallas_call | solution.py:445
  7.8 0.1 collective-permute-start
  7.9 1.8 %collective-permute-done.got = f32[8,13,8,128]{3,2,1,0:T(8,128)S(1)} collective-permute-done((f32[8,13,8,128]{3,2,1,0:T(8,128)S(1)}, f32[8,13,8,128]{3,2,1,0:T(8,128)S(1)}, u32[]{:S(2)}, u32[]{:S(2)}) %collective-permute-start) | collective-permute-done | bytes 426016 | tf_op jit(solution)/shard_map/ppermute | solution.py:466
  9.6 0.1 merge.1
  9.7 4.6 %collective-permute-start.1 = (f32[2,13,8,128]{3,2,1,0:T(8,128)S(1)}, f32[2,13,8,128]{3,2,1,0:T(8,128)S(1)}, u32[]{:S(2)}, u32[]{:S(2)}) collective-permute-start(f32[2,13,8,128]{3,2,1,0:T(8,128)S(1)} %get-tuple-element.20), channel_id=1, source_target_pairs={{0,12},{1,13},{2,14},{3,15},{4,8},{5,9},{6,10},{7,11},{8,4},{9,5},... | collective-permute-start | bytes 319496 | tf_op jit(solution)/shard_map/ppermute | solution.py:476
  14.3 0.0 collective-permute-start.2
  14.3 2.9 %collective-permute-start.3 = (f32[2,13,8,128]{3,2,1,0:T(8,128)S(1)}, f32[2,13,8,128]{3,2,1,0:T(8,128)S(1)}, u32[]{:S(2)}, u32[]{:S(2)}) collective-permute-start(f32[2,13,8,128]{3,2,1,0:T(8,128)S(1)} %get-tuple-element.22), channel_id=1, source_target_pairs={{0,14},{1,15},{2,12},{3,13},{4,10},{5,11},{6,8},{7,9},{8,6},{9,7},... | collective-permute-start | bytes 319496 | tf_op jit(solution)/shard_map/ppermute | solution.py:476
  17.2 1.5 %collective-permute-start.4 = (f32[2,13,8,128]{3,2,1,0:T(8,128)S(1)}, f32[2,13,8,128]{3,2,1,0:T(8,128)S(1)}, u32[]{:S(2)}, u32[]{:S(2)}) collective-permute-start(f32[2,13,8,128]{3,2,1,0:T(8,128)S(1)} %get-tuple-element.23), channel_id=1, source_target_pairs={{0,6},{1,7},{2,4},{3,5},{4,2},{5,3},{6,0},{7,1},{8,14},{9,15},{10,... | collective-permute-start | bytes 319496 | tf_op jit(solution)/shard_map/ppermute | solution.py:476
  18.7 2.4 %collective-permute-start.5 = (f32[2,13,8,128]{3,2,1,0:T(8,128)S(1)}, f32[2,13,8,128]{3,2,1,0:T(8,128)S(1)}, u32[]{:S(2)}, u32[]{:S(2)}) collective-permute-start(f32[2,13,8,128]{3,2,1,0:T(8,128)S(1)} %get-tuple-element.26), channel_id=1, source_target_pairs={{0,10},{1,11},{2,8},{3,9},{4,14},{5,15},{6,12},{7,13},{8,2},{9,3},... | collective-permute-start | bytes 319496 | tf_op jit(solution)/shard_map/ppermute | solution.py:476
  21.1 0.0 collective-permute-done.1.refs_1_
  21.1 4.7 %collective-permute-start.6 = (f32[2,13,8,128]{3,2,1,0:T(8,128)S(1)}, f32[2,13,8,128]{3,2,1,0:T(8,128)S(1)}, u32[]{:S(2)}, u32[]{:S(2)}) collective-permute-start(f32[2,13,8,128]{3,2,1,0:T(8,128)S(1)} %get-tuple-element.27), channel_id=1, source_target_pairs={{0,4},{1,5},{2,6},{3,7},{4,0},{5,1},{6,2},{7,3},{8,12},{9,13},{10,... | collective-permute-start | bytes 319496 | tf_op jit(solution)/shard_map/ppermute | solution.py:476
  25.7 3.2 %collective-permute-done.2.refs_2_ = f32[2,13,8,128]{3,2,1,0:T(8,128)S(1)} collective-permute-done((f32[2,13,8,128]{3,2,1,0:T(8,128)S(1)}, f32[2,13,8,128]{3,2,1,0:T(8,128)S(1)}, u32[]{:S(2)}, u32[]{:S(2)}) %collective-permute-start.2) | collective-permute-done | bytes 106528 | tf_op jit(solution)/shard_map/ppermute | solution.py:476
  29.0 2.1 %collective-permute-start.7 = (f32[2,13,8,128]{3,2,1,0:T(8,128)S(1)}, f32[2,13,8,128]{3,2,1,0:T(8,128)S(1)}, u32[]{:S(2)}, u32[]{:S(2)}) collective-permute-start(f32[2,13,8,128]{3,2,1,0:T(8,128)S(1)} %get-tuple-element.28), channel_id=1, source_target_pairs={{0,2},{1,3},{2,0},{3,1},{4,6},{5,7},{6,4},{7,5},{8,10},{9,11},{10,... | collective-permute-start | bytes 319496 | tf_op jit(solution)/shard_map/ppermute | solution.py:476
  31.1 0.0 collective-permute-done.3.refs_3_
  31.1 0.0 collective-permute-done.4.refs_4_
  31.1 0.0 copy-start
  31.1 0.0 copy-start.1
  31.1 0.0 copy-start.2
  31.1 2.7 %early.1 = (f32[2056,128]{1,0:T(8,128)S(1)}, f32[2056,128]{1,0:T(8,128)S(1)}) custom-call(f32[2,13,8,128]{3,2,1,0:T(8,128)S(1)} %get-tuple-element.19.refs_0_, f32[2,13,8,128]{3,2,1,0:T(8,128)S(1)} %collective-permute-done.1.refs_1_, f32[2,13,8,128]{3,2,1,0:T(8,128)S(1)} %collective-permute-done.2.refs_2_, ...), custom_call_target="tpu_custom_call" | custom-call | flops 3000000000 | bytes 10000000 | tf_op jit(solution)/shard_map/early/pallas_call | solution.py:488
  33.8 0.6 %collective-permute-done.5.refs_2_ = f32[2,13,8,128]{3,2,1,0:T(8,128)S(1)} collective-permute-done((f32[2,13,8,128]{3,2,1,0:T(8,128)S(1)}, f32[2,13,8,128]{3,2,1,0:T(8,128)S(1)}, u32[]{:S(2)}, u32[]{:S(2)}) %collective-permute-start.5) | collective-permute-done | bytes 106528 | tf_op jit(solution)/shard_map/ppermute | solution.py:476
  34.4 0.0 collective-permute-done.6.refs_3_
  34.4 0.9 %collective-permute-done.7.refs_4_ = f32[2,13,8,128]{3,2,1,0:T(8,128)S(1)} collective-permute-done((f32[2,13,8,128]{3,2,1,0:T(8,128)S(1)}, f32[2,13,8,128]{3,2,1,0:T(8,128)S(1)}, u32[]{:S(2)}, u32[]{:S(2)}) %collective-permute-start.7) | collective-permute-done | bytes 106528 | tf_op jit(solution)/shard_map/ppermute | solution.py:476
  35.3 0.0 copy-done
  35.3 0.0 copy-done.1
  35.3 0.0 copy-done.2
  35.3 5.2 %rows.1 = f32[2,128,2,8,128]{4,3,2,1,0:T(8,128)} custom-call(bf16[4,256,256]{2,1,0:T(8,128)(2,1)S(1)} %copy-done, bf16[2,256,256]{2,1,0:T(8,128)(2,1)S(1)} %copy-done.2, f32[2,256,128]{2,1,0:T(8,128)S(1)} %copy-done.1, f32[2056,128]{1,0:T(8,128)S(1)} %get-tuple-element.24.refs_0_, f32[2056,128]{1,0:T(8,128)S(1)} %get-tuple-element.25.refs_1_, ...), custom_call_target="tpu_custom_call" | custom-call | tf_op jit(solution)/shard_map/rows/pallas_call | solution.py:498
Async XLA Ops:
  7.8 1.8 %collective-permute-start = (f32[8,13,8,128]{3,2,1,0:T(8,128)S(1)}, f32[8,13,8,128]{3,2,1,0:T(8,128)S(1)}, u32[]{:S(2)}, u32[]{:S(2)}) collective-permute-start(f32[8,13,8,128]{3,2,1,0:T(8,128)S(1)} %get-tuple-element.18), channel_id=1, source_target_pairs={{0,1},{1,0},{2,3},{3,2},{4,5},{5,4},{6,7},{7,6},{8,9},{9,8},{10,11... | collective-permute-start | bytes 1277960 | tf_op jit(solution)/shard_map/ppermute | solution.py:466
  9.7 11.4 %collective-permute-start.1 = (f32[2,13,8,128]{3,2,1,0:T(8,128)S(1)}, f32[2,13,8,128]{3,2,1,0:T(8,128)S(1)}, u32[]{:S(2)}, u32[]{:S(2)}) collective-permute-start(f32[2,13,8,128]{3,2,1,0:T(8,128)S(1)} %get-tuple-element.20), channel_id=1, source_target_pairs={{0,12},{1,13},{2,14},{3,15},{4,8},{5,9},{6,10},{7,11},{8,4},{9,5},... | collective-permute-start | bytes 319496 | tf_op jit(solution)/shard_map/ppermute | solution.py:476
  14.3 14.7 %collective-permute-start.2 = (f32[2,13,8,128]{3,2,1,0:T(8,128)S(1)}, f32[2,13,8,128]{3,2,1,0:T(8,128)S(1)}, u32[]{:S(2)}, u32[]{:S(2)}) collective-permute-start(f32[2,13,8,128]{3,2,1,0:T(8,128)S(1)} %get-tuple-element.21), channel_id=1, source_target_pairs={{0,8},{1,9},{2,10},{3,11},{4,12},{5,13},{6,14},{7,15},{8,0},{9,1},... | collective-permute-start | bytes 319496 | tf_op jit(solution)/shard_map/ppermute | solution.py:476
  14.3 16.8 %collective-permute-start.3 = (f32[2,13,8,128]{3,2,1,0:T(8,128)S(1)}, f32[2,13,8,128]{3,2,1,0:T(8,128)S(1)}, u32[]{:S(2)}, u32[]{:S(2)}) collective-permute-start(f32[2,13,8,128]{3,2,1,0:T(8,128)S(1)} %get-tuple-element.22), channel_id=1, source_target_pairs={{0,14},{1,15},{2,12},{3,13},{4,10},{5,11},{6,8},{7,9},{8,6},{9,7},... | collective-permute-start | bytes 319496 | tf_op jit(solution)/shard_map/ppermute | solution.py:476
  17.2 13.9 %collective-permute-start.4 = (f32[2,13,8,128]{3,2,1,0:T(8,128)S(1)}, f32[2,13,8,128]{3,2,1,0:T(8,128)S(1)}, u32[]{:S(2)}, u32[]{:S(2)}) collective-permute-start(f32[2,13,8,128]{3,2,1,0:T(8,128)S(1)} %get-tuple-element.23), channel_id=1, source_target_pairs={{0,6},{1,7},{2,4},{3,5},{4,2},{5,3},{6,0},{7,1},{8,14},{9,15},{10,... | collective-permute-start | bytes 319496 | tf_op jit(solution)/shard_map/ppermute | solution.py:476
  18.7 15.7 %collective-permute-start.5 = (f32[2,13,8,128]{3,2,1,0:T(8,128)S(1)}, f32[2,13,8,128]{3,2,1,0:T(8,128)S(1)}, u32[]{:S(2)}, u32[]{:S(2)}) collective-permute-start(f32[2,13,8,128]{3,2,1,0:T(8,128)S(1)} %get-tuple-element.26), channel_id=1, source_target_pairs={{0,10},{1,11},{2,8},{3,9},{4,14},{5,15},{6,12},{7,13},{8,2},{9,3},... | collective-permute-start | bytes 319496 | tf_op jit(solution)/shard_map/ppermute | solution.py:476
  21.1 13.3 %collective-permute-start.6 = (f32[2,13,8,128]{3,2,1,0:T(8,128)S(1)}, f32[2,13,8,128]{3,2,1,0:T(8,128)S(1)}, u32[]{:S(2)}, u32[]{:S(2)}) collective-permute-start(f32[2,13,8,128]{3,2,1,0:T(8,128)S(1)} %get-tuple-element.27), channel_id=1, source_target_pairs={{0,4},{1,5},{2,6},{3,7},{4,0},{5,1},{6,2},{7,3},{8,12},{9,13},{10,... | collective-permute-start | bytes 319496 | tf_op jit(solution)/shard_map/ppermute | solution.py:476
  29.0 6.3 %collective-permute-start.7 = (f32[2,13,8,128]{3,2,1,0:T(8,128)S(1)}, f32[2,13,8,128]{3,2,1,0:T(8,128)S(1)}, u32[]{:S(2)}, u32[]{:S(2)}) collective-permute-start(f32[2,13,8,128]{3,2,1,0:T(8,128)S(1)} %get-tuple-element.28), channel_id=1, source_target_pairs={{0,2},{1,3},{2,0},{3,1},{4,6},{5,7},{6,4},{7,5},{8,10},{9,11},{10,... | collective-permute-start | bytes 319496 | tf_op jit(solution)/shard_map/ppermute | solution.py:476
  31.1 4.2 %copy-start = (bf16[4,256,256]{2,1,0:T(8,128)(2,1)S(1)}, bf16[4,256,256]{2,1,0:T(8,128)(2,1)}, u32[]{:S(2)}) copy-start(bf16[4,256,256]{2,1,0:T(8,128)(2,1)} %constant.21.clone.first) | copy-start | bytes 1572868
  31.1 4.2 %copy-start.1 = (f32[2,256,128]{2,1,0:T(8,128)S(1)}, f32[2,256,128]{2,1,0:T(8,128)}, u32[]{:S(2)}) copy-start(f32[2,256,128]{2,1,0:T(8,128)} %constant.23.clone.twist) | copy-start | bytes 786436
  31.1 4.2 %copy-start.2 = (bf16[2,256,256]{2,1,0:T(8,128)(2,1)S(1)}, bf16[2,256,256]{2,1,0:T(8,128)(2,1)}, u32[]{:S(2)}) copy-start(bf16[2,256,256]{2,1,0:T(8,128)(2,1)} %constant.22.clone.second) | copy-start | bytes 786436

commit v2 on v1

--- a/solution.py
+++ b/solution.py
@@ -113,7 +113,7 @@
     quarter = chips // 4
     far = [k + part for k in range(quarter) for part in (3 * quarter, 2 * quarter)]
     near = list(range(chips // 2 - 1, 0, -1))
-    return [0] + far[:3] + near[:1] + far[3:] + near[1:]
+    return [0] + near[:1] + far + near[1:]
 
 
 def image_kernel(
@@ -351,8 +351,9 @@
                         grids[c][pl.ds(here + 8 * k, 8), :] = before[2 * c + k] + added[2 * c + k]
 
 
-def early_kernel(cap, count, *refs):
-    place_slabs(cap, refs[:count], refs[count : count + 2], refs[count + 2 :])
+def early_kernel(cap, count, started, *refs):
+    earlier, refs = refs[: 2 * started], refs[2 * started :]
+    place_slabs(cap, refs[:count], refs[count : count + 2], refs[count + 2 :], earlier)
 
 
 def row_kernel(
@@ -472,12 +473,14 @@
         compiler_params=pltpu.CompilerParams(vmem_limit_bytes=24 * 1024 * 1024),
         name="merge",
     )(keep, got)
-    received = [messages[0]] + [
-        lax.ppermute(message, "tile", [(source, source ^ (2 * k)) for source in range(owners)])
-        for message, k in zip(messages[1:], exchange_order(owners // 2)[1:])
-    ]
-    early = min(5, owners // 2)
-    late = owners // 2 - early
+    order = exchange_order(owners // 2)
+
+    def exchange(k, message):
+        pairs = [(source, source ^ (2 * k)) for source in range(owners)]
+        return lax.ppermute(message, "tile", pairs) if k else message
+
+    received = [exchange(k, message) for k, message in zip(order, messages)]
+    last = 1 + owners // 4
     grid = jax.ShapeDtypeStruct(((LEAD + 1) * ROWS_DEV, TAIL), jnp.float32)
     placing = [
         pltpu.VMEM((owners, tiles, 8, 128), jnp.float32),
@@ -485,20 +488,24 @@
         pltpu.SMEM((owners, 128), jnp.int32),
         pltpu.SemaphoreType.DMA,
     ]
-    grids = pl.pallas_call(
-        functools.partial(early_kernel, cap, early),
-        out_shape=[grid] * 2,
-        in_specs=[vmem] * early,
-        out_specs=[vmem] * 2,
-        scratch_shapes=placing,
-        cost_estimate=pl.CostEstimate(flops=3 * 10**9, bytes_accessed=10**7, transcendentals=0),
-        compiler_params=pltpu.CompilerParams(vmem_limit_bytes=24 * 1024 * 1024),
-        name="early",
-    )(*received[:early])
+
+    def place_early(grids, stage):
+        return pl.pallas_call(
+            functools.partial(early_kernel, cap, len(stage), len(grids) // 2),
+            out_shape=[grid] * 2,
+            in_specs=[vmem] * (len(grids) + len(stage)),
+            out_specs=[vmem] * 2,
+            scratch_shapes=placing,
+            cost_estimate=pl.CostEstimate(flops=3 * 10**9, bytes_accessed=10**7, transcendentals=0),
+            compiler_params=pltpu.CompilerParams(vmem_limit_bytes=24 * 1024 * 1024),
+            name="early",
+        )(*grids, *stage)
+
+    grids = place_early(place_early([], received[:3]), received[3:last])
     result = pl.pallas_call(
-        functools.partial(row_kernel, cap, late),
+        functools.partial(row_kernel, cap, owners // 2 - last),
         out_shape=jax.ShapeDtypeStruct((2, TAIL, 2, ROWS_DEV, TAIL), jnp.float32),
-        in_specs=[vmem] * (5 + late),
+        in_specs=[vmem] * (5 + owners // 2 - last),
         out_specs=pl.BlockSpec(memory_space=pl.ANY),
         scratch_shapes=[
             *(pltpu.VMEM(grid.shape, grid.dtype) for _ in range(2)),
@@ -509,7 +516,7 @@
         ],
         compiler_params=pltpu.CompilerParams(vmem_limit_bytes=24 * 1024 * 1024),
         name="rows",
-    )(*row_tables(), *grids, *received[early:])
+    )(*row_tables(), *grids, *received[last:])
     return (
         result.reshape(2, LEAD, ROWS_DEV, TAIL).transpose(0, 2, 1, 3).reshape(2, ROWS_DEV, NG)
     )

time: 40.8 us -> 40.5 us (level)
  waiting for transfers between devices: 6.52 us -> 10.8 us
  starting transfers between devices: 18.2 us -> 14.2 us
  Pallas kernels: 15.1 us -> 14.6 us
    ppermute x7, starting transfers between devices: 18.1 us -> 12.5 us  [exchange(): return lax.ppermute(message, 'tile', pairs) if k else message]
    ppermute x7, waiting for transfers between devices: 4.76 us -> 9.37 us  [exchange(): return lax.ppermute(message, 'tile', pairs) if k else message]
    ppermute x1, starting transfers between devices: 0.07 us -> 1.72 us  [shards(): lax.ppermute(give, 'tile', [(source, source ^ 1) for source in range(owne...]
    pallas_call x1, Pallas kernels: 7.15 us -> 5.94 us  [shards(): pl.pallas_call(functools.partial(image_kernel, cap, tile_cols), out_shape...]
    pallas_call x2 -> x3, Pallas kernels: 7.94 us -> 8.55 us  [the longest x1 5.18 us: shards(): pl.pallas_call(functools.partial(row_kernel, cap, owners // 2 - last), ou...]
  transfers between devices with their start and end apart: 8 -> 8, of which waited for: 4 -> 4; matrix products, arithmetic and copies ran while one was open for 0% -> 0% of each run, Pallas kernels for 7% -> 8%
where the time goes in v2:
time: 40.5 us; the launch traced here: 40.2 us
  Pallas kernels  14.6 us (36%)
  starting transfers between devices  14.2 us (35%)
  waiting for transfers between devices  10.8 us (27%)
  between operations  0.71 us (2%)
    ppermute x7, starting transfers between devices, exchange(): return lax.ppermute(message, 'tile', pairs) if k else message  12.5 us
    ppermute x7, waiting for transfers between devices, exchange(): return lax.ppermute(message, 'tile', pairs) if k else message  9.37 us
    pallas_call x1, Pallas kernels, shards(): pl.pallas_call(functools.partial(image_kernel, cap, tile_cols), out_shape...  5.94 us
    pallas_call x1, Pallas kernels, shards(): pl.pallas_call(functools.partial(row_kernel, cap, owners // 2 - last), ou...  5.18 us
    pallas_call x2, Pallas kernels, place_early(): pl.pallas_call(functools.partial(early_kernel, cap, len(stage), len(grids...  3.38 us
    ppermute x1, starting transfers between devices, shards(): lax.ppermute(give, 'tile', [(source, source ^ 1) for source in range(owne...  1.72 us
    ppermute x1, waiting for transfers between devices, shards(): lax.ppermute(give, 'tile', [(source, source ^ 1) for source in range(owne...  1.4 us
  transfers between devices with their start and end apart: 8, of which 4 were waited for; matrix products, arithmetic and copies ran while one was open for 0% of the time, Pallas kernels for 8%

profile of v2, /device:TPU:0, one launch (start us, length us, event | category | flops | bytes accessed | tf_op | source)
XLA Modules:
  0.0 40.2 jit_solution(12173069184174110621)
XLA Ops:
  0.7 5.9 %image.1 = (f32[8,13,8,128]{3,2,1,0:T(8,128)S(1)}, f32[8,13,8,128]{3,2,1,0:T(8,128)S(1)}) custom-call(s32[1]{0:T(128)S(6)} %copy.18.refs_0_, f32[512,16,128]{2,1,0:T(8,128)} %bitcast.14, s32[64]{0:T(128)} %bitcast.18, s32[64]{0:T(128)} %refs_3_.1, s32[64]{0:T(128)} %refs_4_.1, s32[2,64]{1,0:T(2,128)} %bitcast.17, f32[128,128]{1,0:T(8,128)} %bitcast.16, ...), custom_call_target="tpu_custom_call" | custom-call | tf_op jit(solution)/shard_map/image/pallas_call | solution.py:446
  6.6 1.7 %collective-permute-start = (f32[8,13,8,128]{3,2,1,0:T(8,128)S(1)}, f32[8,13,8,128]{3,2,1,0:T(8,128)S(1)}, u32[]{:S(2)}, u32[]{:S(2)}) collective-permute-start(f32[8,13,8,128]{3,2,1,0:T(8,128)S(1)} %get-tuple-element.20), channel_id=1, source_target_pairs={{0,1},{1,0},{2,3},{3,2},{4,5},{5,4},{6,7},{7,6},{8,9},{9,8},{10,11... | collective-permute-start | bytes 1277960 | tf_op jit(solution)/shard_map/ppermute | solution.py:467
  8.3 1.4 %collective-permute-done.got = f32[8,13,8,128]{3,2,1,0:T(8,128)S(1)} collective-permute-done((f32[8,13,8,128]{3,2,1,0:T(8,128)S(1)}, f32[8,13,8,128]{3,2,1,0:T(8,128)S(1)}, u32[]{:S(2)}, u32[]{:S(2)}) %collective-permute-start) | collective-permute-done | bytes 426016 | tf_op jit(solution)/shard_map/ppermute | solution.py:467
  9.7 0.1 merge.1
  9.8 2.8 %collective-permute-start.1 = (f32[2,13,8,128]{3,2,1,0:T(8,128)S(1)}, f32[2,13,8,128]{3,2,1,0:T(8,128)S(1)}, u32[]{:S(2)}, u32[]{:S(2)}) collective-permute-start(f32[2,13,8,128]{3,2,1,0:T(8,128)S(1)} %get-tuple-element.22), channel_id=1, source_target_pairs={{0,6},{1,7},{2,4},{3,5},{4,2},{5,3},{6,0},{7,1},{8,14},{9,15},{10,... | collective-permute-start | bytes 319496 | tf_op jit(solution)/shard_map/ppermute | solution.py:480
  12.6 3.1 %collective-permute-start.2 = (f32[2,13,8,128]{3,2,1,0:T(8,128)S(1)}, f32[2,13,8,128]{3,2,1,0:T(8,128)S(1)}, u32[]{:S(2)}, u32[]{:S(2)}) collective-permute-start(f32[2,13,8,128]{3,2,1,0:T(8,128)S(1)} %get-tuple-element.23), channel_id=1, source_target_pairs={{0,12},{1,13},{2,14},{3,15},{4,8},{5,9},{6,10},{7,11},{8,4},{9,5},... | collective-permute-start | bytes 319496 | tf_op jit(solution)/shard_map/ppermute | solution.py:480
  15.7 0.6 %collective-permute-start.3 = (f32[2,13,8,128]{3,2,1,0:T(8,128)S(1)}, f32[2,13,8,128]{3,2,1,0:T(8,128)S(1)}, u32[]{:S(2)}, u32[]{:S(2)}) collective-permute-start(f32[2,13,8,128]{3,2,1,0:T(8,128)S(1)} %get-tuple-element.26), channel_id=1, source_target_pairs={{0,8},{1,9},{2,10},{3,11},{4,12},{5,13},{6,14},{7,15},{8,0},{9,1},... | collective-permute-start | bytes 319496 | tf_op jit(solution)/shard_map/ppermute | solution.py:480
  16.3 2.3 %collective-permute-start.4 = (f32[2,13,8,128]{3,2,1,0:T(8,128)S(1)}, f32[2,13,8,128]{3,2,1,0:T(8,128)S(1)}, u32[]{:S(2)}, u32[]{:S(2)}) collective-permute-start(f32[2,13,8,128]{3,2,1,0:T(8,128)S(1)} %get-tuple-element.27), channel_id=1, source_target_pairs={{0,14},{1,15},{2,12},{3,13},{4,10},{5,11},{6,8},{7,9},{8,6},{9,7},... | collective-permute-start | bytes 319496 | tf_op jit(solution)/shard_map/ppermute | solution.py:480
  18.7 0.6 %collective-permute-start.5 = (f32[2,13,8,128]{3,2,1,0:T(8,128)S(1)}, f32[2,13,8,128]{3,2,1,0:T(8,128)S(1)}, u32[]{:S(2)}, u32[]{:S(2)}) collective-permute-start(f32[2,13,8,128]{3,2,1,0:T(8,128)S(1)} %get-tuple-element.30), channel_id=1, source_target_pairs={{0,10},{1,11},{2,8},{3,9},{4,14},{5,15},{6,12},{7,13},{8,2},{9,3},... | collective-permute-start | bytes 319496 | tf_op jit(solution)/shard_map/ppermute | solution.py:480
  19.3 0.0 collective-permute-done.1.refs_1_
  19.3 2.3 %collective-permute-start.6 = (f32[2,13,8,128]{3,2,1,0:T(8,128)S(1)}, f32[2,13,8,128]{3,2,1,0:T(8,128)S(1)}, u32[]{:S(2)}, u32[]{:S(2)}) collective-permute-start(f32[2,13,8,128]{3,2,1,0:T(8,128)S(1)} %get-tuple-element.31), channel_id=1, source_target_pairs={{0,4},{1,5},{2,6},{3,7},{4,0},{5,1},{6,2},{7,3},{8,12},{9,13},{10,... | collective-permute-start | bytes 319496 | tf_op jit(solution)/shard_map/ppermute | solution.py:480
  21.6 0.2 collective-permute-done.2.refs_2_
  21.8 0.6 %collective-permute-start.7 = (f32[2,13,8,128]{3,2,1,0:T(8,128)S(1)}, f32[2,13,8,128]{3,2,1,0:T(8,128)S(1)}, u32[]{:S(2)}, u32[]{:S(2)}) collective-permute-start(f32[2,13,8,128]{3,2,1,0:T(8,128)S(1)} %get-tuple-element.32), channel_id=1, source_target_pairs={{0,2},{1,3},{2,0},{3,1},{4,6},{5,7},{6,4},{7,5},{8,10},{9,11},{10,... | collective-permute-start | bytes 319496 | tf_op jit(solution)/shard_map/ppermute | solution.py:480
  22.5 1.9 %early.2 = (f32[2056,128]{1,0:T(8,128)S(1)}, f32[2056,128]{1,0:T(8,128)S(1)}) custom-call(f32[2,13,8,128]{3,2,1,0:T(8,128)S(1)} %get-tuple-element.21.refs_0_, f32[2,13,8,128]{3,2,1,0:T(8,128)S(1)} %collective-permute-done.1.refs_1_, f32[2,13,8,128]{3,2,1,0:T(8,128)S(1)} %collective-permute-done.2.refs_2_), custom_call_target="tpu_custom_call" | custom-call | flops 3000000000 | bytes 10000000 | tf_op jit(solution)/shard_map/early/pallas_call | solution.py:493
  24.4 7.0 %collective-permute-done.3.refs_2_ = f32[2,13,8,128]{3,2,1,0:T(8,128)S(1)} collective-permute-done((f32[2,13,8,128]{3,2,1,0:T(8,128)S(1)}, f32[2,13,8,128]{3,2,1,0:T(8,128)S(1)}, u32[]{:S(2)}, u32[]{:S(2)}) %collective-permute-start.3) | collective-permute-done | bytes 106528 | tf_op jit(solution)/shard_map/ppermute | solution.py:480
  31.4 0.0 collective-permute-done.4.refs_3_
  31.4 0.0 copy-start
  31.4 0.0 copy-start.1
  31.4 0.0 copy-start.2
  31.4 1.4 %early.3 = (f32[2056,128]{1,0:T(8,128)S(1)}, f32[2056,128]{1,0:T(8,128)S(1)}) custom-call(f32[2056,128]{1,0:T(8,128)S(1)} %get-tuple-element.24.refs_0_, f32[2056,128]{1,0:T(8,128)S(1)} %get-tuple-element.25.refs_1_, f32[2,13,8,128]{3,2,1,0:T(8,128)S(1)} %collective-permute-done.3.refs_2_, f32[2,13,8,128]{3,2,1,0:T(8,128)S(1)} %collective-permute-done.4.refs_3_), custom_call_target="tpu_custom_call" | custom-call | flops 3000000000 | bytes 10000000 | tf_op jit(solution)/shard_map/early/pallas_call | solution.py:493
  32.9 2.2 %collective-permute-done.5.refs_2_ = f32[2,13,8,128]{3,2,1,0:T(8,128)S(1)} collective-permute-done((f32[2,13,8,128]{3,2,1,0:T(8,128)S(1)}, f32[2,13,8,128]{3,2,1,0:T(8,128)S(1)}, u32[]{:S(2)}, u32[]{:S(2)}) %collective-permute-start.5) | collective-permute-done | bytes 106528 | tf_op jit(solution)/shard_map/ppermute | solution.py:480
  35.0 0.0 collective-permute-done.6.refs_3_
  35.0 0.0 collective-permute-done.7.refs_4_
  35.0 0.0 copy-done
  35.0 0.0 copy-done.1
  35.1 0.0 copy-done.2
  35.1 5.2 %rows.1 = f32[2,128,2,8,128]{4,3,2,1,0:T(8,128)} custom-call(bf16[4,256,256]{2,1,0:T(8,128)(2,1)S(1)} %copy-done, bf16[2,256,256]{2,1,0:T(8,128)(2,1)S(1)} %copy-done.2, f32[2,256,128]{2,1,0:T(8,128)S(1)} %copy-done.1, f32[2056,128]{1,0:T(8,128)S(1)} %get-tuple-element.28.refs_0_, f32[2056,128]{1,0:T(8,128)S(1)} %get-tuple-element.29.refs_1_, ...), custom_call_target="tpu_custom_call" | custom-call | tf_op jit(solution)/shard_map/rows/pallas_call | solution.py:505
Async XLA Ops:
  6.6 3.1 %collective-permute-start = (f32[8,13,8,128]{3,2,1,0:T(8,128)S(1)}, f32[8,13,8,128]{3,2,1,0:T(8,128)S(1)}, u32[]{:S(2)}, u32[]{:S(2)}) collective-permute-start(f32[8,13,8,128]{3,2,1,0:T(8,128)S(1)} %get-tuple-element.20), channel_id=1, source_target_pairs={{0,1},{1,0},{2,3},{3,2},{4,5},{5,4},{6,7},{7,6},{8,9},{9,8},{10,11... | collective-permute-start | bytes 1277960 | tf_op jit(solution)/shard_map/ppermute | solution.py:467
  9.8 9.5 %collective-permute-start.1 = (f32[2,13,8,128]{3,2,1,0:T(8,128)S(1)}, f32[2,13,8,128]{3,2,1,0:T(8,128)S(1)}, u32[]{:S(2)}, u32[]{:S(2)}) collective-permute-start(f32[2,13,8,128]{3,2,1,0:T(8,128)S(1)} %get-tuple-element.22), channel_id=1, source_target_pairs={{0,6},{1,7},{2,4},{3,5},{4,2},{5,3},{6,0},{7,1},{8,14},{9,15},{10,... | collective-permute-start | bytes 319496 | tf_op jit(solution)/shard_map/ppermute | solution.py:480
  12.6 9.3 %collective-permute-start.2 = (f32[2,13,8,128]{3,2,1,0:T(8,128)S(1)}, f32[2,13,8,128]{3,2,1,0:T(8,128)S(1)}, u32[]{:S(2)}, u32[]{:S(2)}) collective-permute-start(f32[2,13,8,128]{3,2,1,0:T(8,128)S(1)} %get-tuple-element.23), channel_id=1, source_target_pairs={{0,12},{1,13},{2,14},{3,15},{4,8},{5,9},{6,10},{7,11},{8,4},{9,5},... | collective-permute-start | bytes 319496 | tf_op jit(solution)/shard_map/ppermute | solution.py:480
  15.7 15.7 %collective-permute-start.3 = (f32[2,13,8,128]{3,2,1,0:T(8,128)S(1)}, f32[2,13,8,128]{3,2,1,0:T(8,128)S(1)}, u32[]{:S(2)}, u32[]{:S(2)}) collective-permute-start(f32[2,13,8,128]{3,2,1,0:T(8,128)S(1)} %get-tuple-element.26), channel_id=1, source_target_pairs={{0,8},{1,9},{2,10},{3,11},{4,12},{5,13},{6,14},{7,15},{8,0},{9,1},... | collective-permute-start | bytes 319496 | tf_op jit(solution)/shard_map/ppermute | solution.py:480
  16.3 15.1 %collective-permute-start.4 = (f32[2,13,8,128]{3,2,1,0:T(8,128)S(1)}, f32[2,13,8,128]{3,2,1,0:T(8,128)S(1)}, u32[]{:S(2)}, u32[]{:S(2)}) collective-permute-start(f32[2,13,8,128]{3,2,1,0:T(8,128)S(1)} %get-tuple-element.27), channel_id=1, source_target_pairs={{0,14},{1,15},{2,12},{3,13},{4,10},{5,11},{6,8},{7,9},{8,6},{9,7},... | collective-permute-start | bytes 319496 | tf_op jit(solution)/shard_map/ppermute | solution.py:480
  18.7 16.3 %collective-permute-start.5 = (f32[2,13,8,128]{3,2,1,0:T(8,128)S(1)}, f32[2,13,8,128]{3,2,1,0:T(8,128)S(1)}, u32[]{:S(2)}, u32[]{:S(2)}) collective-permute-start(f32[2,13,8,128]{3,2,1,0:T(8,128)S(1)} %get-tuple-element.30), channel_id=1, source_target_pairs={{0,10},{1,11},{2,8},{3,9},{4,14},{5,15},{6,12},{7,13},{8,2},{9,3},... | collective-permute-start | bytes 319496 | tf_op jit(solution)/shard_map/ppermute | solution.py:480
  19.3 15.7 %collective-permute-start.6 = (f32[2,13,8,128]{3,2,1,0:T(8,128)S(1)}, f32[2,13,8,128]{3,2,1,0:T(8,128)S(1)}, u32[]{:S(2)}, u32[]{:S(2)}) collective-permute-start(f32[2,13,8,128]{3,2,1,0:T(8,128)S(1)} %get-tuple-element.31), channel_id=1, source_target_pairs={{0,4},{1,5},{2,6},{3,7},{4,0},{5,1},{6,2},{7,3},{8,12},{9,13},{10,... | collective-permute-start | bytes 319496 | tf_op jit(solution)/shard_map/ppermute | solution.py:480
  21.8 13.2 %collective-permute-start.7 = (f32[2,13,8,128]{3,2,1,0:T(8,128)S(1)}, f32[2,13,8,128]{3,2,1,0:T(8,128)S(1)}, u32[]{:S(2)}, u32[]{:S(2)}) collective-permute-start(f32[2,13,8,128]{3,2,1,0:T(8,128)S(1)} %get-tuple-element.32), channel_id=1, source_target_pairs={{0,2},{1,3},{2,0},{3,1},{4,6},{5,7},{6,4},{7,5},{8,10},{9,11},{10,... | collective-permute-start | bytes 319496 | tf_op jit(solution)/shard_map/ppermute | solution.py:480
  31.4 3.6 %copy-start = (bf16[4,256,256]{2,1,0:T(8,128)(2,1)S(1)}, bf16[4,256,256]{2,1,0:T(8,128)(2,1)}, u32[]{:S(2)}) copy-start(bf16[4,256,256]{2,1,0:T(8,128)(2,1)} %constant.21.clone.first) | copy-start | bytes 1572868
  31.4 3.6 %copy-start.1 = (f32[2,256,128]{2,1,0:T(8,128)S(1)}, f32[2,256,128]{2,1,0:T(8,128)}, u32[]{:S(2)}) copy-start(f32[2,256,128]{2,1,0:T(8,128)} %constant.23.clone.twist) | copy-start | bytes 786436
  31.4 3.6 %copy-start.2 = (bf16[2,256,256]{2,1,0:T(8,128)(2,1)S(1)}, bf16[2,256,256]{2,1,0:T(8,128)(2,1)}, u32[]{:S(2)}) copy-start(bf16[2,256,256]{2,1,0:T(8,128)(2,1)} %constant.22.clone.second) | copy-start | bytes 786436

commit v3 on v2

--- a/solution.py
+++ b/solution.py
@@ -105,8 +105,12 @@
 
 def send_layout(per_device, owners):
     cap = -(-per_device // (owners - SUB // ROWS_DEV + 1))
-    tiles = 2 * cap + (2 * cap + 1 + 3) // 4
+    tiles = 2 * cap + (2 * cap + 3) // 4
     return cap, tiles
+
+
+def merge_halves(cap):
+    return cap % 2
 
 
 def exchange_order(chips):
@@ -134,14 +138,13 @@
     owner_s, row_s, col_s, station_s, vis, coords = copied[:6]
     left_hi, left_lo, right_hi, right_lo, small = copied[6:]
     per_device = vis.shape[0] // 2
-    label_tile = 2 * cap + (2 * cap) // 4
-    label_lane = SUB * ((2 * cap) % 4)
+    label_tile = 2 * cap
     sublane = lax.broadcasted_iota(jnp.int32, (8, 128), 0)
     lane = lax.broadcasted_iota(jnp.int32, (8, 128), 1)
     lane_group = lane // SUB
     out[...] = jnp.zeros_like(out)
-    spread_columns = ((lane - label_lane) * (NG // SUB)).astype(jnp.float32)
-    is_label = (sublane == 0) & (lane >= label_lane) & (lane < label_lane + SUB)
+    spread_columns = (lane * (NG // SUB)).astype(jnp.float32)
+    is_label = (sublane == 7) & (lane < 5 * cap)
     for d in range(owners):
         out[d, label_tile] = jnp.where(is_label, spread_columns, 0.0)
     sky[...] = jnp.zeros_like(sky)
@@ -277,9 +280,9 @@
                 )
             column = jnp.full((8, 128), owner_s[n] * tile_cols + col_s[n], jnp.float32)
             for o in range(5):
-                here = (sublane == 0) & (lane == label_lane + o * cap + rank)
+                here = (sublane == 7) & (lane == o * cap + rank)
                 if o == 4:
-                    here = here & (sublane < shift)
+                    here = here & (sublane - 7 < shift)
                 target = last if o == 4 else band + o
                 pltpu.store(out.at[target ^ me, label_tile], column, mask=here)
 
@@ -301,38 +304,50 @@
         give[k] = out[2 * k + 1]
 
 
-def merge_kernel(keep, got, *messages):
+def merge_kernel(cap, keep, got, *messages):
+    tiles = keep.shape[1]
+    whole = tiles - merge_halves(cap)
+    lane = lax.broadcasted_iota(jnp.int32, (8, 128), 1)
     for k, message in zip(exchange_order(keep.shape[0]), messages):
-        message[0] = keep[k]
-        message[1] = got[k]
+        message[:whole] = keep[k, :whole]
+        message[whole : 2 * whole] = got[k, :whole]
+        if whole < tiles:
+            message[2 * whole] = jnp.where(
+                lane < 64, keep[k, whole], pltpu.roll(got[k, whole], 64, 1)
+            )
 
 
 def place_slabs(cap, messages, grids, scratch, earlier=None):
     received, label_v, label_s, sem = scratch
     sources = 2 * len(messages)
+    whole = received.shape[1] - merge_halves(cap)
     for k, message in enumerate(messages):
-        received[2 * k] = message[0]
-        received[2 * k + 1] = message[1]
-    label_tile = 2 * cap + (2 * cap) // 4
-    label_lane = SUB * ((2 * cap) % 4)
-    label_v[:sources] = received[:sources, label_tile, 0, :].astype(jnp.int32)
+        received[2 * k, :whole] = message[:whole]
+        received[2 * k + 1, :whole] = message[whole : 2 * whole]
+        if merge_halves(cap):
+            received[2 * k, whole] = message[2 * whole]
+            received[2 * k + 1, whole] = pltpu.roll(message[2 * whole], 64, 1)
+    label_v[:sources] = received[:sources, 2 * cap, 7, :].astype(jnp.int32)
     copy = pltpu.make_async_copy(label_v, label_s, sem)
     copy.start()
     for c, grid in enumerate(grids):
         grid[...] = earlier[c][...] if earlier else jnp.zeros_like(grid)
     lane = lax.broadcasted_iota(jnp.int32, (8, 128), 1)
+    not_label = lax.broadcasted_iota(jnp.int32, (8, 128), 0) < 7
     copy.wait()
 
     @pl.loop(0, sources)
     def _(source):
         for i in range(cap):
             for o in range(5):
-                column = label_s[source, label_lane + o * cap + i]
+                column = label_s[source, o * cap + i]
                 offset = column & 127
                 here = pl.multiple_of((column >> 7) * 8, 8)
                 place = lane - offset
                 inside = (place >= 0) & (place < SUB)
                 beyond = place < SUB - 128
+                if o == 4:
+                    inside, beyond = inside & not_label, beyond & not_label
                 added = []
                 for c in range(2):
                     if o < 4:
@@ -466,8 +481,9 @@
     )
     got = lax.ppermute(give, "tile", [(source, source ^ 1) for source in range(owners)])
     messages = pl.pallas_call(
-        merge_kernel,
-        out_shape=[jax.ShapeDtypeStruct((2, tiles, 8, 128), jnp.float32)] * (owners // 2),
+        functools.partial(merge_kernel, cap),
+        out_shape=[jax.ShapeDtypeStruct((2 * tiles - merge_halves(cap), 8, 128), jnp.float32)]
+        * (owners // 2),
         in_specs=[vmem] * 2,
         out_specs=[vmem] * (owners // 2),
         compiler_params=pltpu.CompilerParams(vmem_limit_bytes=24 * 1024 * 1024),

time: 40.5 us -> 39.9 us (0.985)
  Pallas kernels: 14.6 us -> 15.9 us
  starting transfers between devices: 14.2 us -> 12.9 us
  waiting for transfers between devices: 10.8 us -> 10 us
    ppermute x1, starting transfers between devices: 1.72 us -> 0.52 us  [shards(): lax.ppermute(give, 'tile', [(source, source ^ 1) for source in range(owne...]
    pallas_call x1, Pallas kernels: 5.94 us -> 7.13 us  [shards(): pl.pallas_call(functools.partial(image_kernel, cap, tile_cols), out_shape...]
    ppermute x7, waiting for transfers between devices: 9.37 us -> 8.65 us  [exchange(): return lax.ppermute(message, 'tile', pairs) if k else message]
  transfers between devices with their start and end apart: 8 -> 8, of which waited for: 4 -> 4; matrix products, arithmetic and copies ran while one was open for 0% -> 0% of each run, Pallas kernels for 8% -> 9%
where the time goes in v3:
time: 39.9 us; the launch traced here: 39.5 us
  Pallas kernels  15.9 us (40%)
  starting transfers between devices  12.9 us (32%)
  waiting for transfers between devices  10 us (25%)
  between operations  0.71 us (2%)
    ppermute x7, starting transfers between devices, exchange(): return lax.ppermute(message, 'tile', pairs) if k else message  12.3 us
    ppermute x7, waiting for transfers between devices, exchange(): return lax.ppermute(message, 'tile', pairs) if k else message  8.65 us
    pallas_call x1, Pallas kernels, shards(): pl.pallas_call(functools.partial(image_kernel, cap, tile_cols), out_shape...  7.13 us
    pallas_call x1, Pallas kernels, shards(): pl.pallas_call(functools.partial(row_kernel, cap, owners // 2 - last), ou...  5.28 us
    pallas_call x2, Pallas kernels, place_early(): pl.pallas_call(functools.partial(early_kernel, cap, len(stage), len(grids...  3.42 us
    ppermute x1, waiting for transfers between devices, shards(): lax.ppermute(give, 'tile', [(source, source ^ 1) for source in range(owne...  1.4 us
  transfers between devices with their start and end apart: 8, of which 4 were waited for; matrix products, arithmetic and copies ran while one was open for 0% of the time, Pallas kernels for 9%

profile of v3, /device:TPU:0, one launch (start us, length us, event | category | flops | bytes accessed | tf_op | source)
XLA Modules:
  0.0 39.5 jit_solution(16188207805616662207)
XLA Ops:
  0.7 7.1 %image.1 = (f32[8,13,8,128]{3,2,1,0:T(8,128)S(1)}, f32[8,13,8,128]{3,2,1,0:T(8,128)S(1)}) custom-call(s32[1]{0:T(128)S(6)} %copy.18.refs_0_, f32[512,16,128]{2,1,0:T(8,128)} %bitcast.14, s32[64]{0:T(128)} %bitcast.18, s32[64]{0:T(128)} %refs_3_.1, s32[64]{0:T(128)} %refs_4_.1, s32[2,64]{1,0:T(2,128)} %bitcast.17, f32[128,128]{1,0:T(8,128)} %bitcast.16, ...), custom_call_target="tpu_custom_call" | custom-call | tf_op jit(solution)/shard_map/image/pallas_call | solution.py:461
  7.8 0.5 %collective-permute-start = (f32[8,13,8,128]{3,2,1,0:T(8,128)S(1)}, f32[8,13,8,128]{3,2,1,0:T(8,128)S(1)}, u32[]{:S(2)}, u32[]{:S(2)}) collective-permute-start(f32[8,13,8,128]{3,2,1,0:T(8,128)S(1)} %get-tuple-element.20), channel_id=1, source_target_pairs={{0,1},{1,0},{2,3},{3,2},{4,5},{5,4},{6,7},{7,6},{8,9},{9,8},{10,11... | collective-permute-start | bytes 1277960 | tf_op jit(solution)/shard_map/ppermute | solution.py:482
  8.3 1.4 %collective-permute-done.got = f32[8,13,8,128]{3,2,1,0:T(8,128)S(1)} collective-permute-done((f32[8,13,8,128]{3,2,1,0:T(8,128)S(1)}, f32[8,13,8,128]{3,2,1,0:T(8,128)S(1)}, u32[]{:S(2)}, u32[]{:S(2)}) %collective-permute-start) | collective-permute-done | bytes 426016 | tf_op jit(solution)/shard_map/ppermute | solution.py:482
  9.7 0.1 merge.1
  9.8 2.8 %collective-permute-start.1 = (f32[25,8,128]{2,1,0:T(8,128)S(1)}, f32[25,8,128]{2,1,0:T(8,128)S(1)}, u32[]{:S(2)}, u32[]{:S(2)}) collective-permute-start(f32[25,8,128]{2,1,0:T(8,128)S(1)} %get-tuple-element.22), channel_id=1, source_target_pairs={{0,6},{1,7},{2,4},{3,5},{4,2},{5,3},{6,0},{7,1},{8,14},{9,15},{10,... | collective-permute-start | bytes 307208 | tf_op jit(solution)/shard_map/ppermute | solution.py:496
  12.5 3.7 %collective-permute-start.2 = (f32[25,8,128]{2,1,0:T(8,128)S(1)}, f32[25,8,128]{2,1,0:T(8,128)S(1)}, u32[]{:S(2)}, u32[]{:S(2)}) collective-permute-start(f32[25,8,128]{2,1,0:T(8,128)S(1)} %get-tuple-element.23), channel_id=1, source_target_pairs={{0,12},{1,13},{2,14},{3,15},{4,8},{5,9},{6,10},{7,11},{8,4},{9,5},... | collective-permute-start | bytes 307208 | tf_op jit(solution)/shard_map/ppermute | solution.py:496
  16.2 0.1 collective-permute-start.3
  16.3 2.3 %collective-permute-start.4 = (f32[25,8,128]{2,1,0:T(8,128)S(1)}, f32[25,8,128]{2,1,0:T(8,128)S(1)}, u32[]{:S(2)}, u32[]{:S(2)}) collective-permute-start(f32[25,8,128]{2,1,0:T(8,128)S(1)} %get-tuple-element.27), channel_id=1, source_target_pairs={{0,14},{1,15},{2,12},{3,13},{4,10},{5,11},{6,8},{7,9},{8,6},{9,7},... | collective-permute-start | bytes 307208 | tf_op jit(solution)/shard_map/ppermute | solution.py:496
  18.7 0.6 %collective-permute-start.5 = (f32[25,8,128]{2,1,0:T(8,128)S(1)}, f32[25,8,128]{2,1,0:T(8,128)S(1)}, u32[]{:S(2)}, u32[]{:S(2)}) collective-permute-start(f32[25,8,128]{2,1,0:T(8,128)S(1)} %get-tuple-element.30), channel_id=1, source_target_pairs={{0,10},{1,11},{2,8},{3,9},{4,14},{5,15},{6,12},{7,13},{8,2},{9,3},... | collective-permute-start | bytes 307208 | tf_op jit(solution)/shard_map/ppermute | solution.py:496
  19.3 0.0 collective-permute-done.1.refs_1_
  19.3 2.3 %collective-permute-start.6 = (f32[25,8,128]{2,1,0:T(8,128)S(1)}, f32[25,8,128]{2,1,0:T(8,128)S(1)}, u32[]{:S(2)}, u32[]{:S(2)}) collective-permute-start(f32[25,8,128]{2,1,0:T(8,128)S(1)} %get-tuple-element.31), channel_id=1, source_target_pairs={{0,4},{1,5},{2,6},{3,7},{4,0},{5,1},{6,2},{7,3},{8,12},{9,13},{10,... | collective-permute-start | bytes 307208 | tf_op jit(solution)/shard_map/ppermute | solution.py:496
  21.6 0.6 %collective-permute-done.2.refs_2_ = f32[25,8,128]{2,1,0:T(8,128)S(1)} collective-permute-done((f32[25,8,128]{2,1,0:T(8,128)S(1)}, f32[25,8,128]{2,1,0:T(8,128)S(1)}, u32[]{:S(2)}, u32[]{:S(2)}) %collective-permute-start.2) | collective-permute-done | bytes 102432 | tf_op jit(solution)/shard_map/ppermute | solution.py:496
  22.2 0.5 %collective-permute-start.7 = (f32[25,8,128]{2,1,0:T(8,128)S(1)}, f32[25,8,128]{2,1,0:T(8,128)S(1)}, u32[]{:S(2)}, u32[]{:S(2)}) collective-permute-start(f32[25,8,128]{2,1,0:T(8,128)S(1)} %get-tuple-element.32), channel_id=1, source_target_pairs={{0,2},{1,3},{2,0},{3,1},{4,6},{5,7},{6,4},{7,5},{8,10},{9,11},{10,... | collective-permute-start | bytes 307208 | tf_op jit(solution)/shard_map/ppermute | solution.py:496
  22.7 2.0 %early.2 = (f32[2056,128]{1,0:T(8,128)S(1)}, f32[2056,128]{1,0:T(8,128)S(1)}) custom-call(f32[25,8,128]{2,1,0:T(8,128)S(1)} %get-tuple-element.21.refs_0_, f32[25,8,128]{2,1,0:T(8,128)S(1)} %collective-permute-done.1.refs_1_, f32[25,8,128]{2,1,0:T(8,128)S(1)} %collective-permute-done.2.refs_2_), custom_call_target="tpu_custom_call" | custom-call | flops 3000000000 | bytes 10000000 | tf_op jit(solution)/shard_map/early/pallas_call | solution.py:509
  24.7 5.9 %collective-permute-done.3.refs_2_ = f32[25,8,128]{2,1,0:T(8,128)S(1)} collective-permute-done((f32[25,8,128]{2,1,0:T(8,128)S(1)}, f32[25,8,128]{2,1,0:T(8,128)S(1)}, u32[]{:S(2)}, u32[]{:S(2)}) %collective-permute-start.3) | collective-permute-done | bytes 102432 | tf_op jit(solution)/shard_map/ppermute | solution.py:496
  30.6 0.0 collective-permute-done.4.refs_3_
  30.6 0.0 copy-start
  30.6 0.0 copy-start.1
  30.6 0.0 copy-start.2
  30.6 1.5 %early.3 = (f32[2056,128]{1,0:T(8,128)S(1)}, f32[2056,128]{1,0:T(8,128)S(1)}) custom-call(f32[2056,128]{1,0:T(8,128)S(1)} %get-tuple-element.24.refs_0_, f32[2056,128]{1,0:T(8,128)S(1)} %get-tuple-element.25.refs_1_, f32[25,8,128]{2,1,0:T(8,128)S(1)} %collective-permute-done.3.refs_2_, f32[25,8,128]{2,1,0:T(8,128)S(1)} %collective-permute-done.4.refs_3_), custom_call_target="tpu_custom_call" | custom-call | flops 3000000000 | bytes 10000000 | tf_op jit(solution)/shard_map/early/pallas_call | solution.py:509
  32.1 2.2 %collective-permute-done.5.refs_2_ = f32[25,8,128]{2,1,0:T(8,128)S(1)} collective-permute-done((f32[25,8,128]{2,1,0:T(8,128)S(1)}, f32[25,8,128]{2,1,0:T(8,128)S(1)}, u32[]{:S(2)}, u32[]{:S(2)}) %collective-permute-start.5) | collective-permute-done | bytes 102432 | tf_op jit(solution)/shard_map/ppermute | solution.py:496
  34.2 0.0 collective-permute-done.6.refs_3_
  34.2 0.0 collective-permute-done.7.refs_4_
  34.2 0.0 copy-done
  34.2 0.0 copy-done.1
  34.2 0.0 copy-done.2
  34.3 5.3 %rows.1 = f32[2,128,2,8,128]{4,3,2,1,0:T(8,128)} custom-call(bf16[4,256,256]{2,1,0:T(8,128)(2,1)S(1)} %copy-done, bf16[2,256,256]{2,1,0:T(8,128)(2,1)S(1)} %copy-done.2, f32[2,256,128]{2,1,0:T(8,128)S(1)} %copy-done.1, f32[2056,128]{1,0:T(8,128)S(1)} %get-tuple-element.28.refs_0_, f32[2056,128]{1,0:T(8,128)S(1)} %get-tuple-element.29.refs_1_, ...), custom_call_target="tpu_custom_call" | custom-call | tf_op jit(solution)/shard_map/rows/pallas_call | solution.py:521
Async XLA Ops:
  7.8 1.9 %collective-permute-start = (f32[8,13,8,128]{3,2,1,0:T(8,128)S(1)}, f32[8,13,8,128]{3,2,1,0:T(8,128)S(1)}, u32[]{:S(2)}, u32[]{:S(2)}) collective-permute-start(f32[8,13,8,128]{3,2,1,0:T(8,128)S(1)} %get-tuple-element.20), channel_id=1, source_target_pairs={{0,1},{1,0},{2,3},{3,2},{4,5},{5,4},{6,7},{7,6},{8,9},{9,8},{10,11... | collective-permute-start | bytes 1277960 | tf_op jit(solution)/shard_map/ppermute | solution.py:482
  9.8 9.5 %collective-permute-start.1 = (f32[25,8,128]{2,1,0:T(8,128)S(1)}, f32[25,8,128]{2,1,0:T(8,128)S(1)}, u32[]{:S(2)}, u32[]{:S(2)}) collective-permute-start(f32[25,8,128]{2,1,0:T(8,128)S(1)} %get-tuple-element.22), channel_id=1, source_target_pairs={{0,6},{1,7},{2,4},{3,5},{4,2},{5,3},{6,0},{7,1},{8,14},{9,15},{10,... | collective-permute-start | bytes 307208 | tf_op jit(solution)/shard_map/ppermute | solution.py:496
  12.5 9.7 %collective-permute-start.2 = (f32[25,8,128]{2,1,0:T(8,128)S(1)}, f32[25,8,128]{2,1,0:T(8,128)S(1)}, u32[]{:S(2)}, u32[]{:S(2)}) collective-permute-start(f32[25,8,128]{2,1,0:T(8,128)S(1)} %get-tuple-element.23), channel_id=1, source_target_pairs={{0,12},{1,13},{2,14},{3,15},{4,8},{5,9},{6,10},{7,11},{8,4},{9,5},... | collective-permute-start | bytes 307208 | tf_op jit(solution)/shard_map/ppermute | solution.py:496
  16.2 14.4 %collective-permute-start.3 = (f32[25,8,128]{2,1,0:T(8,128)S(1)}, f32[25,8,128]{2,1,0:T(8,128)S(1)}, u32[]{:S(2)}, u32[]{:S(2)}) collective-permute-start(f32[25,8,128]{2,1,0:T(8,128)S(1)} %get-tuple-element.26), channel_id=1, source_target_pairs={{0,8},{1,9},{2,10},{3,11},{4,12},{5,13},{6,14},{7,15},{8,0},{9,1},... | collective-permute-start | bytes 307208 | tf_op jit(solution)/shard_map/ppermute | solution.py:496
  16.3 14.3 %collective-permute-start.4 = (f32[25,8,128]{2,1,0:T(8,128)S(1)}, f32[25,8,128]{2,1,0:T(8,128)S(1)}, u32[]{:S(2)}, u32[]{:S(2)}) collective-permute-start(f32[25,8,128]{2,1,0:T(8,128)S(1)} %get-tuple-element.27), channel_id=1, source_target_pairs={{0,14},{1,15},{2,12},{3,13},{4,10},{5,11},{6,8},{7,9},{8,6},{9,7},... | collective-permute-start | bytes 307208 | tf_op jit(solution)/shard_map/ppermute | solution.py:496
  18.7 15.6 %collective-permute-start.5 = (f32[25,8,128]{2,1,0:T(8,128)S(1)}, f32[25,8,128]{2,1,0:T(8,128)S(1)}, u32[]{:S(2)}, u32[]{:S(2)}) collective-permute-start(f32[25,8,128]{2,1,0:T(8,128)S(1)} %get-tuple-element.30), channel_id=1, source_target_pairs={{0,10},{1,11},{2,8},{3,9},{4,14},{5,15},{6,12},{7,13},{8,2},{9,3},... | collective-permute-start | bytes 307208 | tf_op jit(solution)/shard_map/ppermute | solution.py:496
  19.3 14.9 %collective-permute-start.6 = (f32[25,8,128]{2,1,0:T(8,128)S(1)}, f32[25,8,128]{2,1,0:T(8,128)S(1)}, u32[]{:S(2)}, u32[]{:S(2)}) collective-permute-start(f32[25,8,128]{2,1,0:T(8,128)S(1)} %get-tuple-element.31), channel_id=1, source_target_pairs={{0,4},{1,5},{2,6},{3,7},{4,0},{5,1},{6,2},{7,3},{8,12},{9,13},{10,... | collective-permute-start | bytes 307208 | tf_op jit(solution)/shard_map/ppermute | solution.py:496
  22.2 12.0 %collective-permute-start.7 = (f32[25,8,128]{2,1,0:T(8,128)S(1)}, f32[25,8,128]{2,1,0:T(8,128)S(1)}, u32[]{:S(2)}, u32[]{:S(2)}) collective-permute-start(f32[25,8,128]{2,1,0:T(8,128)S(1)} %get-tuple-element.32), channel_id=1, source_target_pairs={{0,2},{1,3},{2,0},{3,1},{4,6},{5,7},{6,4},{7,5},{8,10},{9,11},{10,... | collective-permute-start | bytes 307208 | tf_op jit(solution)/shard_map/ppermute | solution.py:496
  30.6 3.7 %copy-start = (bf16[4,256,256]{2,1,0:T(8,128)(2,1)S(1)}, bf16[4,256,256]{2,1,0:T(8,128)(2,1)}, u32[]{:S(2)}) copy-start(bf16[4,256,256]{2,1,0:T(8,128)(2,1)} %constant.21.clone.first) | copy-start | bytes 1572868
  30.6 3.7 %copy-start.1 = (f32[2,256,128]{2,1,0:T(8,128)S(1)}, f32[2,256,128]{2,1,0:T(8,128)}, u32[]{:S(2)}) copy-start(f32[2,256,128]{2,1,0:T(8,128)} %constant.23.clone.twist) | copy-start | bytes 786436
  30.6 3.7 %copy-start.2 = (bf16[2,256,256]{2,1,0:T(8,128)(2,1)S(1)}, bf16[2,256,256]{2,1,0:T(8,128)(2,1)}, u32[]{:S(2)}) copy-start(bf16[2,256,256]{2,1,0:T(8,128)(2,1)} %constant.22.clone.second) | copy-start | bytes 786436

commit v4 on v3

--- a/solution.py
+++ b/solution.py
@@ -117,7 +117,7 @@
     quarter = chips // 4
     far = [k + part for k in range(quarter) for part in (3 * quarter, 2 * quarter)]
     near = list(range(chips // 2 - 1, 0, -1))
-    return [0] + near[:1] + far + near[1:]
+    return [0] + far[:1] + near[:1] + far[1:] + near[1:]
 
 
 def image_kernel(

time: 39.9 us -> 38.8 us (0.972)
  starting transfers between devices: 12.9 us -> 14.5 us
  Pallas kernels: 15.9 us -> 14.7 us
  waiting for transfers between devices: 10 us -> 8.8 us
    ppermute x7, waiting for transfers between devices: 8.65 us -> 7.41 us  [exchange(): return lax.ppermute(message, 'tile', pairs) if k else message]
    ppermute x1, starting transfers between devices: 0.52 us -> 1.71 us  [shards(): lax.ppermute(give, 'tile', [(source, source ^ 1) for source in range(owne...]
    pallas_call x1, Pallas kernels: 7.13 us -> 5.94 us  [shards(): pl.pallas_call(functools.partial(image_kernel, cap, tile_cols), out_shape...]
    ppermute x7, starting transfers between devices: 12.3 us -> 12.8 us  [exchange(): return lax.ppermute(message, 'tile', pairs) if k else message]
where the time goes in v4:
time: 38.8 us
  Pallas kernels  14.7 us (38%)
  starting transfers between devices  14.5 us (37%)
  waiting for transfers between devices  8.8 us (23%)
  between operations  0.71 us (2%)
    ppermute x7, starting transfers between devices, exchange(): return lax.ppermute(message, 'tile', pairs) if k else message  12.8 us
    ppermute x7, waiting for transfers between devices, exchange(): return lax.ppermute(message, 'tile', pairs) if k else message  7.41 us
    pallas_call x1, Pallas kernels, shards(): pl.pallas_call(functools.partial(image_kernel, cap, tile_cols), out_shape...  5.94 us
    pallas_call x1, Pallas kernels, shards(): pl.pallas_call(functools.partial(row_kernel, cap, owners // 2 - last), ou...  5.29 us
    pallas_call x2, Pallas kernels, place_early(): pl.pallas_call(functools.partial(early_kernel, cap, len(stage), len(grids...  3.42 us
    ppermute x1, starting transfers between devices, shards(): lax.ppermute(give, 'tile', [(source, source ^ 1) for source in range(owne...  1.71 us
    ppermute x1, waiting for transfers between devices, shards(): lax.ppermute(give, 'tile', [(source, source ^ 1) for source in range(owne...  1.4 us
  transfers between devices with their start and end apart: 8, of which 4 were waited for; matrix products, arithmetic and copies ran while one was open for 0% of the time, Pallas kernels for 9%

profile of v4, /device:TPU:0, one launch (start us, length us, event | category | flops | bytes accessed | tf_op | source)
XLA Modules:
  0.0 38.8 jit_solution(2933107454125639638)
XLA Ops:
  0.7 5.9 %image.1 = (f32[8,13,8,128]{3,2,1,0:T(8,128)S(1)}, f32[8,13,8,128]{3,2,1,0:T(8,128)S(1)}) custom-call(s32[1]{0:T(128)S(6)} %copy.18.refs_0_, f32[512,16,128]{2,1,0:T(8,128)} %bitcast.14, s32[64]{0:T(128)} %bitcast.18, s32[64]{0:T(128)} %refs_3_.1, s32[64]{0:T(128)} %refs_4_.1, s32[2,64]{1,0:T(2,128)} %bitcast.17, f32[128,128]{1,0:T(8,128)} %bitcast.16, ...), custom_call_target="tpu_custom_call" | custom-call | tf_op jit(solution)/shard_map/image/pallas_call | solution.py:461
  6.6 1.7 %collective-permute-start = (f32[8,13,8,128]{3,2,1,0:T(8,128)S(1)}, f32[8,13,8,128]{3,2,1,0:T(8,128)S(1)}, u32[]{:S(2)}, u32[]{:S(2)}) collective-permute-start(f32[8,13,8,128]{3,2,1,0:T(8,128)S(1)} %get-tuple-element.20), channel_id=1, source_target_pairs={{0,1},{1,0},{2,3},{3,2},{4,5},{5,4},{6,7},{7,6},{8,9},{9,8},{10,11... | collective-permute-start | bytes 1277960 | tf_op jit(solution)/shard_map/ppermute | solution.py:482
  8.3 1.4 %collective-permute-done.got = f32[8,13,8,128]{3,2,1,0:T(8,128)S(1)} collective-permute-done((f32[8,13,8,128]{3,2,1,0:T(8,128)S(1)}, f32[8,13,8,128]{3,2,1,0:T(8,128)S(1)}, u32[]{:S(2)}, u32[]{:S(2)}) %collective-permute-start) | collective-permute-done | bytes 426016 | tf_op jit(solution)/shard_map/ppermute | solution.py:482
  9.7 0.1 merge.1
  9.8 5.0 %collective-permute-start.1 = (f32[25,8,128]{2,1,0:T(8,128)S(1)}, f32[25,8,128]{2,1,0:T(8,128)S(1)}, u32[]{:S(2)}, u32[]{:S(2)}) collective-permute-start(f32[25,8,128]{2,1,0:T(8,128)S(1)} %get-tuple-element.22), channel_id=1, source_target_pairs={{0,12},{1,13},{2,14},{3,15},{4,8},{5,9},{6,10},{7,11},{8,4},{9,5},... | collective-permute-start | bytes 307208 | tf_op jit(solution)/shard_map/ppermute | solution.py:496
  14.8 0.5 %collective-permute-start.2 = (f32[25,8,128]{2,1,0:T(8,128)S(1)}, f32[25,8,128]{2,1,0:T(8,128)S(1)}, u32[]{:S(2)}, u32[]{:S(2)}) collective-permute-start(f32[25,8,128]{2,1,0:T(8,128)S(1)} %get-tuple-element.23), channel_id=1, source_target_pairs={{0,6},{1,7},{2,4},{3,5},{4,2},{5,3},{6,0},{7,1},{8,14},{9,15},{10,... | collective-permute-start | bytes 307208 | tf_op jit(solution)/shard_map/ppermute | solution.py:496
  15.3 0.7 %collective-permute-start.3 = (f32[25,8,128]{2,1,0:T(8,128)S(1)}, f32[25,8,128]{2,1,0:T(8,128)S(1)}, u32[]{:S(2)}, u32[]{:S(2)}) collective-permute-start(f32[25,8,128]{2,1,0:T(8,128)S(1)} %get-tuple-element.26), channel_id=1, source_target_pairs={{0,8},{1,9},{2,10},{3,11},{4,12},{5,13},{6,14},{7,15},{8,0},{9,1},... | collective-permute-start | bytes 307208 | tf_op jit(solution)/shard_map/ppermute | solution.py:496
  16.0 4.1 %collective-permute-start.4 = (f32[25,8,128]{2,1,0:T(8,128)S(1)}, f32[25,8,128]{2,1,0:T(8,128)S(1)}, u32[]{:S(2)}, u32[]{:S(2)}) collective-permute-start(f32[25,8,128]{2,1,0:T(8,128)S(1)} %get-tuple-element.27), channel_id=1, source_target_pairs={{0,14},{1,15},{2,12},{3,13},{4,10},{5,11},{6,8},{7,9},{8,6},{9,7},... | collective-permute-start | bytes 307208 | tf_op jit(solution)/shard_map/ppermute | solution.py:496
  20.1 0.0 collective-permute-start.5
  20.1 0.0 collective-permute-done.1.refs_1_
  20.1 1.2 %collective-permute-start.6 = (f32[25,8,128]{2,1,0:T(8,128)S(1)}, f32[25,8,128]{2,1,0:T(8,128)S(1)}, u32[]{:S(2)}, u32[]{:S(2)}) collective-permute-start(f32[25,8,128]{2,1,0:T(8,128)S(1)} %get-tuple-element.31), channel_id=1, source_target_pairs={{0,4},{1,5},{2,6},{3,7},{4,0},{5,1},{6,2},{7,3},{8,12},{9,13},{10,... | collective-permute-start | bytes 307208 | tf_op jit(solution)/shard_map/ppermute | solution.py:496
  21.3 0.1 collective-permute-done.2.refs_2_
  21.5 1.3 %collective-permute-start.7 = (f32[25,8,128]{2,1,0:T(8,128)S(1)}, f32[25,8,128]{2,1,0:T(8,128)S(1)}, u32[]{:S(2)}, u32[]{:S(2)}) collective-permute-start(f32[25,8,128]{2,1,0:T(8,128)S(1)} %get-tuple-element.32), channel_id=1, source_target_pairs={{0,2},{1,3},{2,0},{3,1},{4,6},{5,7},{6,4},{7,5},{8,10},{9,11},{10,... | collective-permute-start | bytes 307208 | tf_op jit(solution)/shard_map/ppermute | solution.py:496
  22.7 2.0 %early.2 = (f32[2056,128]{1,0:T(8,128)S(1)}, f32[2056,128]{1,0:T(8,128)S(1)}) custom-call(f32[25,8,128]{2,1,0:T(8,128)S(1)} %get-tuple-element.21.refs_0_, f32[25,8,128]{2,1,0:T(8,128)S(1)} %collective-permute-done.1.refs_1_, f32[25,8,128]{2,1,0:T(8,128)S(1)} %collective-permute-done.2.refs_2_), custom_call_target="tpu_custom_call" | custom-call | flops 3000000000 | bytes 10000000 | tf_op jit(solution)/shard_map/early/pallas_call | solution.py:509
  24.7 4.2 %collective-permute-done.3.refs_2_ = f32[25,8,128]{2,1,0:T(8,128)S(1)} collective-permute-done((f32[25,8,128]{2,1,0:T(8,128)S(1)}, f32[25,8,128]{2,1,0:T(8,128)S(1)}, u32[]{:S(2)}, u32[]{:S(2)}) %collective-permute-start.3) | collective-permute-done | bytes 102432 | tf_op jit(solution)/shard_map/ppermute | solution.py:496
  29.0 0.0 collective-permute-done.4.refs_3_
  29.0 0.0 copy-start
  29.0 0.0 copy-start.1
  29.0 0.0 copy-start.2
  29.0 1.5 %early.3 = (f32[2056,128]{1,0:T(8,128)S(1)}, f32[2056,128]{1,0:T(8,128)S(1)}) custom-call(f32[2056,128]{1,0:T(8,128)S(1)} %get-tuple-element.24.refs_0_, f32[2056,128]{1,0:T(8,128)S(1)} %get-tuple-element.25.refs_1_, f32[25,8,128]{2,1,0:T(8,128)S(1)} %collective-permute-done.3.refs_2_, f32[25,8,128]{2,1,0:T(8,128)S(1)} %collective-permute-done.4.refs_3_), custom_call_target="tpu_custom_call" | custom-call | flops 3000000000 | bytes 10000000 | tf_op jit(solution)/shard_map/early/pallas_call | solution.py:509
  30.4 3.0 %collective-permute-done.5.refs_2_ = f32[25,8,128]{2,1,0:T(8,128)S(1)} collective-permute-done((f32[25,8,128]{2,1,0:T(8,128)S(1)}, f32[25,8,128]{2,1,0:T(8,128)S(1)}, u32[]{:S(2)}, u32[]{:S(2)}) %collective-permute-start.5) | collective-permute-done | bytes 102432 | tf_op jit(solution)/shard_map/ppermute | solution.py:496
  33.5 0.0 collective-permute-done.6.refs_3_
  33.5 0.0 collective-permute-done.7.refs_4_
  33.5 0.0 copy-done
  33.5 0.0 copy-done.1
  33.5 0.0 copy-done.2
  33.5 5.3 %rows.1 = f32[2,128,2,8,128]{4,3,2,1,0:T(8,128)} custom-call(bf16[4,256,256]{2,1,0:T(8,128)(2,1)S(1)} %copy-done, bf16[2,256,256]{2,1,0:T(8,128)(2,1)S(1)} %copy-done.2, f32[2,256,128]{2,1,0:T(8,128)S(1)} %copy-done.1, f32[2056,128]{1,0:T(8,128)S(1)} %get-tuple-element.28.refs_0_, f32[2056,128]{1,0:T(8,128)S(1)} %get-tuple-element.29.refs_1_, ...), custom_call_target="tpu_custom_call" | custom-call | tf_op jit(solution)/shard_map/rows/pallas_call | solution.py:521
Async XLA Ops:
  6.6 3.1 %collective-permute-start = (f32[8,13,8,128]{3,2,1,0:T(8,128)S(1)}, f32[8,13,8,128]{3,2,1,0:T(8,128)S(1)}, u32[]{:S(2)}, u32[]{:S(2)}) collective-permute-start(f32[8,13,8,128]{3,2,1,0:T(8,128)S(1)} %get-tuple-element.20), channel_id=1, source_target_pairs={{0,1},{1,0},{2,3},{3,2},{4,5},{5,4},{6,7},{7,6},{8,9},{9,8},{10,11... | collective-permute-start | bytes 1277960 | tf_op jit(solution)/shard_map/ppermute | solution.py:482
  9.8 10.3 %collective-permute-start.1 = (f32[25,8,128]{2,1,0:T(8,128)S(1)}, f32[25,8,128]{2,1,0:T(8,128)S(1)}, u32[]{:S(2)}, u32[]{:S(2)}) collective-permute-start(f32[25,8,128]{2,1,0:T(8,128)S(1)} %get-tuple-element.22), channel_id=1, source_target_pairs={{0,12},{1,13},{2,14},{3,15},{4,8},{5,9},{6,10},{7,11},{8,4},{9,5},... | collective-permute-start | bytes 307208 | tf_op jit(solution)/shard_map/ppermute | solution.py:496
  14.8 6.6 %collective-permute-start.2 = (f32[25,8,128]{2,1,0:T(8,128)S(1)}, f32[25,8,128]{2,1,0:T(8,128)S(1)}, u32[]{:S(2)}, u32[]{:S(2)}) collective-permute-start(f32[25,8,128]{2,1,0:T(8,128)S(1)} %get-tuple-element.23), channel_id=1, source_target_pairs={{0,6},{1,7},{2,4},{3,5},{4,2},{5,3},{6,0},{7,1},{8,14},{9,15},{10,... | collective-permute-start | bytes 307208 | tf_op jit(solution)/shard_map/ppermute | solution.py:496
  15.3 13.6 %collective-permute-start.3 = (f32[25,8,128]{2,1,0:T(8,128)S(1)}, f32[25,8,128]{2,1,0:T(8,128)S(1)}, u32[]{:S(2)}, u32[]{:S(2)}) collective-permute-start(f32[25,8,128]{2,1,0:T(8,128)S(1)} %get-tuple-element.26), channel_id=1, source_target_pairs={{0,8},{1,9},{2,10},{3,11},{4,12},{5,13},{6,14},{7,15},{8,0},{9,1},... | collective-permute-start | bytes 307208 | tf_op jit(solution)/shard_map/ppermute | solution.py:496
  16.0 12.9 %collective-permute-start.4 = (f32[25,8,128]{2,1,0:T(8,128)S(1)}, f32[25,8,128]{2,1,0:T(8,128)S(1)}, u32[]{:S(2)}, u32[]{:S(2)}) collective-permute-start(f32[25,8,128]{2,1,0:T(8,128)S(1)} %get-tuple-element.27), channel_id=1, source_target_pairs={{0,14},{1,15},{2,12},{3,13},{4,10},{5,11},{6,8},{7,9},{8,6},{9,7},... | collective-permute-start | bytes 307208 | tf_op jit(solution)/shard_map/ppermute | solution.py:496
  20.1 13.4 %collective-permute-start.5 = (f32[25,8,128]{2,1,0:T(8,128)S(1)}, f32[25,8,128]{2,1,0:T(8,128)S(1)}, u32[]{:S(2)}, u32[]{:S(2)}) collective-permute-start(f32[25,8,128]{2,1,0:T(8,128)S(1)} %get-tuple-element.30), channel_id=1, source_target_pairs={{0,10},{1,11},{2,8},{3,9},{4,14},{5,15},{6,12},{7,13},{8,2},{9,3},... | collective-permute-start | bytes 307208 | tf_op jit(solution)/shard_map/ppermute | solution.py:496
  20.1 13.4 %collective-permute-start.6 = (f32[25,8,128]{2,1,0:T(8,128)S(1)}, f32[25,8,128]{2,1,0:T(8,128)S(1)}, u32[]{:S(2)}, u32[]{:S(2)}) collective-permute-start(f32[25,8,128]{2,1,0:T(8,128)S(1)} %get-tuple-element.31), channel_id=1, source_target_pairs={{0,4},{1,5},{2,6},{3,7},{4,0},{5,1},{6,2},{7,3},{8,12},{9,13},{10,... | collective-permute-start | bytes 307208 | tf_op jit(solution)/shard_map/ppermute | solution.py:496
  21.5 12.0 %collective-permute-start.7 = (f32[25,8,128]{2,1,0:T(8,128)S(1)}, f32[25,8,128]{2,1,0:T(8,128)S(1)}, u32[]{:S(2)}, u32[]{:S(2)}) collective-permute-start(f32[25,8,128]{2,1,0:T(8,128)S(1)} %get-tuple-element.32), channel_id=1, source_target_pairs={{0,2},{1,3},{2,0},{3,1},{4,6},{5,7},{6,4},{7,5},{8,10},{9,11},{10,... | collective-permute-start | bytes 307208 | tf_op jit(solution)/shard_map/ppermute | solution.py:496
  29.0 4.5 %copy-start = (bf16[4,256,256]{2,1,0:T(8,128)(2,1)S(1)}, bf16[4,256,256]{2,1,0:T(8,128)(2,1)}, u32[]{:S(2)}) copy-start(bf16[4,256,256]{2,1,0:T(8,128)(2,1)} %constant.21.clone.first) | copy-start | bytes 1572868
  29.0 4.5 %copy-start.1 = (f32[2,256,128]{2,1,0:T(8,128)S(1)}, f32[2,256,128]{2,1,0:T(8,128)}, u32[]{:S(2)}) copy-start(f32[2,256,128]{2,1,0:T(8,128)} %constant.23.clone.twist) | copy-start | bytes 786436
  29.0 4.5 %copy-start.2 = (bf16[2,256,256]{2,1,0:T(8,128)(2,1)S(1)}, bf16[2,256,256]{2,1,0:T(8,128)(2,1)}, u32[]{:S(2)}) copy-start(bf16[2,256,256]{2,1,0:T(8,128)(2,1)} %constant.22.clone.second) | copy-start | bytes 786436

commit v5 on v4

--- a/solution.py
+++ b/solution.py
@@ -116,7 +116,7 @@
 def exchange_order(chips):
     quarter = chips // 4
     far = [k + part for k in range(quarter) for part in (3 * quarter, 2 * quarter)]
-    near = list(range(chips // 2 - 1, 0, -1))
+    near = [1] + list(range(chips // 2 - 1, 1, -1))
     return [0] + far[:1] + near[:1] + far[1:] + near[1:]
 
 

time: 38.8 us -> 39.5 us (1.018)
  starting transfers between devices: 14.5 us -> 20.2 us
  waiting for transfers between devices: 8.8 us -> 3.84 us
    ppermute x7, starting transfers between devices: 12.8 us -> 19.6 us  [exchange(): return lax.ppermute(message, 'tile', pairs) if k else message]
    ppermute x7, waiting for transfers between devices: 7.41 us -> 2.44 us  [exchange(): return lax.ppermute(message, 'tile', pairs) if k else message]
    ppermute x1, starting transfers between devices: 1.71 us -> 0.52 us  [shards(): lax.ppermute(give, 'tile', [(source, source ^ 1) for source in range(owne...]
  transfers between devices with their start and end apart: 8 -> 8, of which waited for: 4 -> 3; matrix products, arithmetic and copies ran while one was open for 0% -> 0% of each run, Pallas kernels for 9% -> 9%
where the time goes in v5:
time: 39.5 us
  starting transfers between devices  20.2 us (51%)
  Pallas kernels  14.7 us (37%)
  waiting for transfers between devices  3.84 us (10%)
  between operations  0.73 us (2%)
    ppermute x7, starting transfers between devices, exchange(): return lax.ppermute(message, 'tile', pairs) if k else message  19.6 us
    pallas_call x1, Pallas kernels, shards(): pl.pallas_call(functools.partial(image_kernel, cap, tile_cols), out_shape...  5.94 us
    pallas_call x1, Pallas kernels, shards(): pl.pallas_call(functools.partial(row_kernel, cap, owners // 2 - last), ou...  5.28 us
    pallas_call x2, Pallas kernels, place_early(): pl.pallas_call(functools.partial(early_kernel, cap, len(stage), len(grids...  3.42 us
    ppermute x7, waiting for transfers between devices, exchange(): return lax.ppermute(message, 'tile', pairs) if k else message  2.44 us
    ppermute x1, waiting for transfers between devices, shards(): lax.ppermute(give, 'tile', [(source, source ^ 1) for source in range(owne...  1.4 us
  transfers between devices with their start and end apart: 8, of which 3 were waited for; matrix products, arithmetic and copies ran while one was open for 0% of the time, Pallas kernels for 9%

profile of v5, /device:TPU:0, one launch (start us, length us, event | category | flops | bytes accessed | tf_op | source)
XLA Modules:
  0.0 39.5 jit_solution(10440012402313593013)
XLA Ops:
  0.7 5.9 %image.1 = (f32[8,13,8,128]{3,2,1,0:T(8,128)S(1)}, f32[8,13,8,128]{3,2,1,0:T(8,128)S(1)}) custom-call(s32[1]{0:T(128)S(6)} %copy.18.refs_0_, f32[512,16,128]{2,1,0:T(8,128)} %bitcast.14, s32[64]{0:T(128)} %bitcast.18, s32[64]{0:T(128)} %refs_3_.1, s32[64]{0:T(128)} %refs_4_.1, s32[2,64]{1,0:T(2,128)} %bitcast.17, f32[128,128]{1,0:T(8,128)} %bitcast.16, ...), custom_call_target="tpu_custom_call" | custom-call | tf_op jit(solution)/shard_map/image/pallas_call | solution.py:461
  6.6 0.5 %collective-permute-start = (f32[8,13,8,128]{3,2,1,0:T(8,128)S(1)}, f32[8,13,8,128]{3,2,1,0:T(8,128)S(1)}, u32[]{:S(2)}, u32[]{:S(2)}) collective-permute-start(f32[8,13,8,128]{3,2,1,0:T(8,128)S(1)} %get-tuple-element.20), channel_id=1, source_target_pairs={{0,1},{1,0},{2,3},{3,2},{4,5},{5,4},{6,7},{7,6},{8,9},{9,8},{10,11... | collective-permute-start | bytes 1277960 | tf_op jit(solution)/shard_map/ppermute | solution.py:482
  7.1 1.4 %collective-permute-done.got = f32[8,13,8,128]{3,2,1,0:T(8,128)S(1)} collective-permute-done((f32[8,13,8,128]{3,2,1,0:T(8,128)S(1)}, f32[8,13,8,128]{3,2,1,0:T(8,128)S(1)}, u32[]{:S(2)}, u32[]{:S(2)}) %collective-permute-start) | collective-permute-done | bytes 426016 | tf_op jit(solution)/shard_map/ppermute | solution.py:482
  8.5 0.1 merge.1
  8.6 6.2 %collective-permute-start.1 = (f32[25,8,128]{2,1,0:T(8,128)S(1)}, f32[25,8,128]{2,1,0:T(8,128)S(1)}, u32[]{:S(2)}, u32[]{:S(2)}) collective-permute-start(f32[25,8,128]{2,1,0:T(8,128)S(1)} %get-tuple-element.22), channel_id=1, source_target_pairs={{0,12},{1,13},{2,14},{3,15},{4,8},{5,9},{6,10},{7,11},{8,4},{9,5},... | collective-permute-start | bytes 307208 | tf_op jit(solution)/shard_map/ppermute | solution.py:496
  14.8 0.3 collective-permute-start.2
  15.1 0.6 %collective-permute-start.3 = (f32[25,8,128]{2,1,0:T(8,128)S(1)}, f32[25,8,128]{2,1,0:T(8,128)S(1)}, u32[]{:S(2)}, u32[]{:S(2)}) collective-permute-start(f32[25,8,128]{2,1,0:T(8,128)S(1)} %get-tuple-element.26), channel_id=1, source_target_pairs={{0,8},{1,9},{2,10},{3,11},{4,12},{5,13},{6,14},{7,15},{8,0},{9,1},... | collective-permute-start | bytes 307208 | tf_op jit(solution)/shard_map/ppermute | solution.py:496
  15.8 2.4 %collective-permute-start.4 = (f32[25,8,128]{2,1,0:T(8,128)S(1)}, f32[25,8,128]{2,1,0:T(8,128)S(1)}, u32[]{:S(2)}, u32[]{:S(2)}) collective-permute-start(f32[25,8,128]{2,1,0:T(8,128)S(1)} %get-tuple-element.27), channel_id=1, source_target_pairs={{0,14},{1,15},{2,12},{3,13},{4,10},{5,11},{6,8},{7,9},{8,6},{9,7},... | collective-permute-start | bytes 307208 | tf_op jit(solution)/shard_map/ppermute | solution.py:496
  18.2 1.3 %collective-permute-start.5 = (f32[25,8,128]{2,1,0:T(8,128)S(1)}, f32[25,8,128]{2,1,0:T(8,128)S(1)}, u32[]{:S(2)}, u32[]{:S(2)}) collective-permute-start(f32[25,8,128]{2,1,0:T(8,128)S(1)} %get-tuple-element.30), channel_id=1, source_target_pairs={{0,10},{1,11},{2,8},{3,9},{4,14},{5,15},{6,12},{7,13},{8,2},{9,3},... | collective-permute-start | bytes 307208 | tf_op jit(solution)/shard_map/ppermute | solution.py:496
  19.5 0.0 collective-permute-done.1.refs_1_
  19.5 8.8 %collective-permute-start.6 = (f32[25,8,128]{2,1,0:T(8,128)S(1)}, f32[25,8,128]{2,1,0:T(8,128)S(1)}, u32[]{:S(2)}, u32[]{:S(2)}) collective-permute-start(f32[25,8,128]{2,1,0:T(8,128)S(1)} %get-tuple-element.31), channel_id=1, source_target_pairs={{0,6},{1,7},{2,4},{3,5},{4,2},{5,3},{6,0},{7,1},{8,14},{9,15},{10,... | collective-permute-start | bytes 307208 | tf_op jit(solution)/shard_map/ppermute | solution.py:496
  28.2 0.0 collective-permute-done.2.refs_2_
  28.2 0.0 collective-permute-start.7
  28.2 2.0 %early.2 = (f32[2056,128]{1,0:T(8,128)S(1)}, f32[2056,128]{1,0:T(8,128)S(1)}) custom-call(f32[25,8,128]{2,1,0:T(8,128)S(1)} %get-tuple-element.21.refs_0_, f32[25,8,128]{2,1,0:T(8,128)S(1)} %collective-permute-done.1.refs_1_, f32[25,8,128]{2,1,0:T(8,128)S(1)} %collective-permute-done.2.refs_2_), custom_call_target="tpu_custom_call" | custom-call | flops 3000000000 | bytes 10000000 | tf_op jit(solution)/shard_map/early/pallas_call | solution.py:509
  30.2 0.0 collective-permute-done.3.refs_2_
  30.2 0.0 collective-permute-done.4.refs_3_
  30.2 0.0 copy-start
  30.2 0.0 copy-start.1
  30.3 0.0 copy-start.2
  30.3 1.5 %early.3 = (f32[2056,128]{1,0:T(8,128)S(1)}, f32[2056,128]{1,0:T(8,128)S(1)}) custom-call(f32[2056,128]{1,0:T(8,128)S(1)} %get-tuple-element.24.refs_0_, f32[2056,128]{1,0:T(8,128)S(1)} %get-tuple-element.25.refs_1_, f32[25,8,128]{2,1,0:T(8,128)S(1)} %collective-permute-done.3.refs_2_, f32[25,8,128]{2,1,0:T(8,128)S(1)} %collective-permute-done.4.refs_3_), custom_call_target="tpu_custom_call" | custom-call | flops 3000000000 | bytes 10000000 | tf_op jit(solution)/shard_map/early/pallas_call | solution.py:509
  31.7 1.8 %collective-permute-done.5.refs_2_ = f32[25,8,128]{2,1,0:T(8,128)S(1)} collective-permute-done((f32[25,8,128]{2,1,0:T(8,128)S(1)}, f32[25,8,128]{2,1,0:T(8,128)S(1)}, u32[]{:S(2)}, u32[]{:S(2)}) %collective-permute-start.5) | collective-permute-done | bytes 102432 | tf_op jit(solution)/shard_map/ppermute | solution.py:496
  33.6 0.6 %collective-permute-done.6.refs_3_ = f32[25,8,128]{2,1,0:T(8,128)S(1)} collective-permute-done((f32[25,8,128]{2,1,0:T(8,128)S(1)}, f32[25,8,128]{2,1,0:T(8,128)S(1)}, u32[]{:S(2)}, u32[]{:S(2)}) %collective-permute-start.6) | collective-permute-done | bytes 102432 | tf_op jit(solution)/shard_map/ppermute | solution.py:496
  34.2 0.0 collective-permute-done.7.refs_4_
  34.2 0.0 copy-done
  34.2 0.0 copy-done.1
  34.2 0.0 copy-done.2
  34.2 5.3 %rows.1 = f32[2,128,2,8,128]{4,3,2,1,0:T(8,128)} custom-call(bf16[4,256,256]{2,1,0:T(8,128)(2,1)S(1)} %copy-done, bf16[2,256,256]{2,1,0:T(8,128)(2,1)S(1)} %copy-done.2, f32[2,256,128]{2,1,0:T(8,128)S(1)} %copy-done.1, f32[2056,128]{1,0:T(8,128)S(1)} %get-tuple-element.28.refs_0_, f32[2056,128]{1,0:T(8,128)S(1)} %get-tuple-element.29.refs_1_, ...), custom_call_target="tpu_custom_call" | custom-call | tf_op jit(solution)/shard_map/rows/pallas_call | solution.py:521
Async XLA Ops:
  6.6 1.9 %collective-permute-start = (f32[8,13,8,128]{3,2,1,0:T(8,128)S(1)}, f32[8,13,8,128]{3,2,1,0:T(8,128)S(1)}, u32[]{:S(2)}, u32[]{:S(2)}) collective-permute-start(f32[8,13,8,128]{3,2,1,0:T(8,128)S(1)} %get-tuple-element.20), channel_id=1, source_target_pairs={{0,1},{1,0},{2,3},{3,2},{4,5},{5,4},{6,7},{7,6},{8,9},{9,8},{10,11... | collective-permute-start | bytes 1277960 | tf_op jit(solution)/shard_map/ppermute | solution.py:482
  8.6 10.9 %collective-permute-start.1 = (f32[25,8,128]{2,1,0:T(8,128)S(1)}, f32[25,8,128]{2,1,0:T(8,128)S(1)}, u32[]{:S(2)}, u32[]{:S(2)}) collective-permute-start(f32[25,8,128]{2,1,0:T(8,128)S(1)} %get-tuple-element.22), channel_id=1, source_target_pairs={{0,12},{1,13},{2,14},{3,15},{4,8},{5,9},{6,10},{7,11},{8,4},{9,5},... | collective-permute-start | bytes 307208 | tf_op jit(solution)/shard_map/ppermute | solution.py:496
  14.8 13.4 %collective-permute-start.2 = (f32[25,8,128]{2,1,0:T(8,128)S(1)}, f32[25,8,128]{2,1,0:T(8,128)S(1)}, u32[]{:S(2)}, u32[]{:S(2)}) collective-permute-start(f32[25,8,128]{2,1,0:T(8,128)S(1)} %get-tuple-element.23), channel_id=1, source_target_pairs={{0,2},{1,3},{2,0},{3,1},{4,6},{5,7},{6,4},{7,5},{8,10},{9,11},{10,... | collective-permute-start | bytes 307208 | tf_op jit(solution)/shard_map/ppermute | solution.py:496
  15.1 15.1 %collective-permute-start.3 = (f32[25,8,128]{2,1,0:T(8,128)S(1)}, f32[25,8,128]{2,1,0:T(8,128)S(1)}, u32[]{:S(2)}, u32[]{:S(2)}) collective-permute-start(f32[25,8,128]{2,1,0:T(8,128)S(1)} %get-tuple-element.26), channel_id=1, source_target_pairs={{0,8},{1,9},{2,10},{3,11},{4,12},{5,13},{6,14},{7,15},{8,0},{9,1},... | collective-permute-start | bytes 307208 | tf_op jit(solution)/shard_map/ppermute | solution.py:496
  15.8 14.5 %collective-permute-start.4 = (f32[25,8,128]{2,1,0:T(8,128)S(1)}, f32[25,8,128]{2,1,0:T(8,128)S(1)}, u32[]{:S(2)}, u32[]{:S(2)}) collective-permute-start(f32[25,8,128]{2,1,0:T(8,128)S(1)} %get-tuple-element.27), channel_id=1, source_target_pairs={{0,14},{1,15},{2,12},{3,13},{4,10},{5,11},{6,8},{7,9},{8,6},{9,7},... | collective-permute-start | bytes 307208 | tf_op jit(solution)/shard_map/ppermute | solution.py:496
  18.2 15.4 %collective-permute-start.5 = (f32[25,8,128]{2,1,0:T(8,128)S(1)}, f32[25,8,128]{2,1,0:T(8,128)S(1)}, u32[]{:S(2)}, u32[]{:S(2)}) collective-permute-start(f32[25,8,128]{2,1,0:T(8,128)S(1)} %get-tuple-element.30), channel_id=1, source_target_pairs={{0,10},{1,11},{2,8},{3,9},{4,14},{5,15},{6,12},{7,13},{8,2},{9,3},... | collective-permute-start | bytes 307208 | tf_op jit(solution)/shard_map/ppermute | solution.py:496
  19.5 14.7 %collective-permute-start.6 = (f32[25,8,128]{2,1,0:T(8,128)S(1)}, f32[25,8,128]{2,1,0:T(8,128)S(1)}, u32[]{:S(2)}, u32[]{:S(2)}) collective-permute-start(f32[25,8,128]{2,1,0:T(8,128)S(1)} %get-tuple-element.31), channel_id=1, source_target_pairs={{0,6},{1,7},{2,4},{3,5},{4,2},{5,3},{6,0},{7,1},{8,14},{9,15},{10,... | collective-permute-start | bytes 307208 | tf_op jit(solution)/shard_map/ppermute | solution.py:496
  28.2 5.9 %collective-permute-start.7 = (f32[25,8,128]{2,1,0:T(8,128)S(1)}, f32[25,8,128]{2,1,0:T(8,128)S(1)}, u32[]{:S(2)}, u32[]{:S(2)}) collective-permute-start(f32[25,8,128]{2,1,0:T(8,128)S(1)} %get-tuple-element.32), channel_id=1, source_target_pairs={{0,4},{1,5},{2,6},{3,7},{4,0},{5,1},{6,2},{7,3},{8,12},{9,13},{10,... | collective-permute-start | bytes 307208 | tf_op jit(solution)/shard_map/ppermute | solution.py:496
  30.2 3.9 %copy-start = (bf16[4,256,256]{2,1,0:T(8,128)(2,1)S(1)}, bf16[4,256,256]{2,1,0:T(8,128)(2,1)}, u32[]{:S(2)}) copy-start(bf16[4,256,256]{2,1,0:T(8,128)(2,1)} %constant.21.clone.first) | copy-start | bytes 1572868
  30.2 3.9 %copy-start.1 = (f32[2,256,128]{2,1,0:T(8,128)S(1)}, f32[2,256,128]{2,1,0:T(8,128)}, u32[]{:S(2)}) copy-start(f32[2,256,128]{2,1,0:T(8,128)} %constant.23.clone.twist) | copy-start | bytes 786436
  30.3 3.9 %copy-start.2 = (bf16[2,256,256]{2,1,0:T(8,128)(2,1)S(1)}, bf16[2,256,256]{2,1,0:T(8,128)(2,1)}, u32[]{:S(2)}) copy-start(bf16[2,256,256]{2,1,0:T(8,128)(2,1)} %constant.22.clone.second) | copy-start | bytes 786436
